TPU v7x, 512 devices: a whole 4x4x16 slice. The times are simulated.
512 devices in a mesh: batch: 16 (over y, x_lo, core), fsdp: 32 (over z, x_hi).
Axes of the slice: x: 4 (x_hi: 2, x_lo: 2; x = x_hi * 2 + x_lo), y: 4, z: 16, core: 2. Of those that a mesh axis runs over, the one named last changes fastest.
Arguments:
- queries: bfloat16 [1024, 4096], P(('batch', 'fsdp')), may hold values from -1 to 1
- passages: bfloat16 [1024, 4096], P(('batch', 'fsdp')), may hold values from -0.5 to 0.5
- positives: int32 [1024], P(('batch', 'fsdp')), may hold values from 0 to 1023
- hidden: bfloat16 [1024, 256, 4096], P(('batch', 'fsdp')), may hold values from -6 to 6
- norm_gain: bfloat16 [4096], replicated, may hold values from 0.5 to 1.5
- last_query: bfloat16 [1024, 2048], P(('batch', 'fsdp')), may hold values from -6 to 6
- frozen_key_weight: bfloat16 [4096, 512], P('fsdp'), may hold values from -0.09375 to 0.09375
- frozen_value_weight: bfloat16 [4096, 512], P('fsdp'), may hold values from -0.09375 to 0.09375
- key_down: bfloat16 [4096, 64], P('fsdp'), may hold values from -0.09375 to 0.09375
- key_adapter_up: bfloat16 [64, 512], replicated, may hold values from -0.75 to 0.75
- value_down: bfloat16 [4096, 64], P('fsdp'), may hold values from -0.09375 to 0.09375
- value_adapter_up: bfloat16 [64, 512], replicated, may hold values from -0.75 to 0.75
- out_weight: bfloat16 [2048, 4096], P('batch', 'fsdp'), may hold values from -0.125 to 0.125
Outputs:
- losses: float32 [1024], P(('batch', 'fsdp'))
- query_embedding_gradient: float32 [1024, 4096], P(('batch', 'fsdp'))
- passage_embedding_gradient: float32 [1024, 4096], P(('batch', 'fsdp'))
- key_down_grad: float32 [4096, 64], P(('batch', 'fsdp'))
- value_down_grad: float32 [4096, 64], P(('batch', 'fsdp'))
- key_up_grad: float32 [64, 512], replicated
- value_up_grad: float32 [64, 512], replicated
All inputs are finite; a program needn't handle non-finite values.
Results may differ from a plain program's by a relative error of at most 0.02.
Values may be sent and summed in bfloat16 or wider, within the bound.
A program may use at most 64 MiB of HBM per device.

v0:
```python
import jax
import jax.numpy as jnp
from jax import lax
from jax.sharding import PartitionSpec as P

HEAD_WIDTH = 128


INVERSE_TEMP_SCL = 20.0
ADAPTER_SCALE = 2.0
EPSILON = 1e-06
ROTARY_BASE = 1000000.0


def rotary_tables(length, head_size):
    half_size = head_size // 2
    position = jnp.arange(length, dtype=jnp.float32)
    frequency = ROTARY_BASE ** (-(jnp.arange(half_size, dtype=jnp.float32) * 2.0 / head_size))
    angles = position[:, None] * frequency[None, :]
    return (jnp.cos(angles)[:, None, :], jnp.sin(angles)[:, None, :])


def encode_backward(
    tokens,
    query_vec,
    grad_vec,
    norm_gain,
    frozen_key_weight,
    frozen_value_weight,
    key_down,
    key_adapter_up,
    value_down,
    value_adapter_up,
):
    length = tokens.shape[0]
    head_size = HEAD_WIDTH
    kv_width = frozen_key_weight.shape[1]
    groups = kv_width // head_size
    group_size = query_vec.shape[0] // kv_width
    tokens_wide = tokens.astype(jnp.float32)
    normed = (
        tokens_wide
        * lax.rsqrt(jnp.mean(tokens_wide * tokens_wide, axis=-1, keepdims=True) + EPSILON)
        * norm_gain.astype(jnp.float32)
    ).astype(jnp.bfloat16)
    low_key = jnp.dot(normed, key_down, preferred_element_type=jnp.float32).astype(jnp.bfloat16)
    low_value = jnp.dot(normed, value_down, preferred_element_type=jnp.float32).astype(jnp.bfloat16)
    key_rows = jnp.dot(
        normed, frozen_key_weight, preferred_element_type=jnp.float32
    ) + ADAPTER_SCALE * jnp.dot(low_key, key_adapter_up, preferred_element_type=jnp.float32)
    key_rows = key_rows.reshape(length, groups, head_size)
    cosine, sine = rotary_tables(length, head_size)
    leading = key_rows[..., : head_size // 2]
    trailing = key_rows[..., head_size // 2 :]
    key_rows = jnp.concatenate(
        [leading * cosine - trailing * sine, trailing * cosine + leading * sine], axis=-1
    ).astype(jnp.bfloat16)
    values = (
        jnp.dot(normed, frozen_value_weight, preferred_element_type=jnp.float32)
        + ADAPTER_SCALE * jnp.dot(low_value, value_adapter_up, preferred_element_type=jnp.float32)
    ).astype(jnp.bfloat16)
    values = values.reshape(length, groups, head_size)
    query_heads = query_vec.astype(jnp.float32).reshape(groups, group_size, head_size)
    similarity_scores = jnp.einsum(
        "gjd,tgd->gjt", query_heads, key_rows.astype(jnp.float32)
    ) * head_size ** (-0.5)
    attention = jax.nn.softmax(similarity_scores, axis=-1)
    grad_heads = grad_vec.astype(jnp.float32).reshape(groups, group_size, head_size)
    prob_grad = jnp.einsum("gjd,tgd->gjt", grad_heads, values.astype(jnp.float32))
    expected = jnp.sum(attention * prob_grad, axis=-1, keepdims=True)
    score_grad = attention * (prob_grad - expected)
    value_grad = jnp.einsum("gjt,gjd->tgd", attention, grad_heads)
    rotated_grad = jnp.einsum("gjt,gjd->tgd", score_grad, query_heads) * head_size ** (-0.5)
    grad_lead = rotated_grad[..., : head_size // 2]
    grad_trail = rotated_grad[..., head_size // 2 :]
    key_grad = jnp.concatenate(
        [grad_lead * cosine + grad_trail * sine, grad_trail * cosine - grad_lead * sine], axis=-1
    )
    key_cast = key_grad.reshape(length, kv_width).astype(jnp.bfloat16)
    value_cast = value_grad.reshape(length, kv_width).astype(jnp.bfloat16)
    contract = (((0,), (0,)), ((), ()))
    up_key = ADAPTER_SCALE * lax.dot_general(
        low_key, key_cast, contract, preferred_element_type=jnp.float32
    )
    up_value = ADAPTER_SCALE * lax.dot_general(
        low_value, value_cast, contract, preferred_element_type=jnp.float32
    )
    back_key = jnp.dot(key_cast, key_adapter_up.T, preferred_element_type=jnp.float32).astype(
        jnp.bfloat16
    )
    back_value = jnp.dot(value_cast, value_adapter_up.T, preferred_element_type=jnp.float32).astype(
        jnp.bfloat16
    )
    down_key = ADAPTER_SCALE * lax.dot_general(
        normed, back_key, contract, preferred_element_type=jnp.float32
    )
    down_value = ADAPTER_SCALE * lax.dot_general(
        normed, back_value, contract, preferred_element_type=jnp.float32
    )
    return (down_key, down_value, up_key, up_value)


def tile_scores(query_block, passage_block, position_block, passage_ids):
    similarity_scores = INVERSE_TEMP_SCL * jnp.dot(
        query_block, passage_block.T, preferred_element_type=jnp.float32
    )
    onehot = (position_block[:, None] == passage_ids[None, :]).astype(jnp.float32)
    return (similarity_scores, onehot)


def tile_finish(row_max, exponent, denominator, positive, onehot, own_start, pair_count):
    log_total = row_max + jnp.log(denominator)
    losses = lax.dynamic_slice_in_dim(log_total - positive, own_start, pair_count, 0)
    softmax_weights = (exponent / denominator[:, None] - onehot).astype(jnp.bfloat16)
    return (losses, softmax_weights)


def shards(
    queries,
    passages,
    positives,
    hidden,
    norm_gain,
    last_query,
    frozen_key_weight,
    frozen_value_weight,
    key_down,
    key_adapter_up,
    value_down,
    value_adapter_up,
    out_weight,
):
    pair_count = queries.shape[0]
    passage_count = hidden.shape[0]
    batch_size = lax.axis_size("batch")
    fsdp_size = lax.axis_size("fsdp")
    fsdp_index = lax.axis_index("fsdp")
    contract = (((0,), (0,)), ((), ()))
    query_block, position_block = (
        lax.all_gather(queries, "fsdp", axis=0, tiled=True),
        lax.all_gather(positives, "fsdp", axis=0, tiled=True),
    )
    passage_block = lax.all_gather(passages, "batch", axis=0, tiled=True)
    slot_ids = jnp.arange(batch_size * pair_count, dtype=jnp.int32)
    passage_ids = (
        slot_ids // pair_count * fsdp_size + fsdp_index
    ) * pair_count + slot_ids % pair_count
    similarity_scores, onehot = tile_scores(query_block, passage_block, position_block, passage_ids)
    row_max = lax.pmax(jnp.max(similarity_scores, axis=1), "fsdp")
    exponent = jnp.exp(similarity_scores - row_max[:, None])
    denominator, positive = lax.psum(
        (jnp.sum(exponent, axis=1), jnp.sum(similarity_scores * onehot, axis=1)), "fsdp"
    )
    losses, softmax_weights = tile_finish(
        row_max, exponent, denominator, positive, onehot, fsdp_index * pair_count, pair_count
    )
    query_loss_part = INVERSE_TEMP_SCL * jnp.dot(
        softmax_weights, passage_block, preferred_element_type=jnp.float32
    )
    query_embedding_gradient = lax.psum_scatter(
        query_loss_part.astype(jnp.bfloat16), "fsdp", scatter_dimension=0, tiled=True
    ).astype(jnp.float32)
    passage_loss_part = INVERSE_TEMP_SCL * lax.dot_general(
        softmax_weights, query_block, contract, preferred_element_type=jnp.float32
    )
    passage_embedding_gradient = lax.psum_scatter(
        passage_loss_part, "batch", scatter_dimension=0, tiled=True
    )
    key_full, value_full, key_first, value_first = (
        lax.all_gather(frozen_key_weight, "fsdp", axis=0, tiled=True),
        lax.all_gather(frozen_value_weight, "fsdp", axis=0, tiled=True),
        lax.all_gather(key_down, "fsdp", axis=0, tiled=True),
        lax.all_gather(value_down, "fsdp", axis=0, tiled=True),
    )
    width_block = passage_embedding_gradient.shape[1] // fsdp_size
    stride = pair_count // passage_count
    own_grad = passage_embedding_gradient.astype(jnp.bfloat16).reshape(
        passage_count, fsdp_size, width_block
    )
    grad_blocks = lax.all_to_all(own_grad, "fsdp", split_axis=1, concat_axis=0, tiled=True)
    grad_rows = grad_blocks.reshape(fsdp_size * passage_count, width_block)
    output_block = lax.all_gather(out_weight, "batch", axis=0, tiled=True)
    head_part = lax.dot_general(
        grad_rows, output_block, (((1,), (1,)), ((), ())), preferred_element_type=jnp.float32
    )
    head_total = lax.psum_scatter(head_part, "fsdp", scatter_dimension=0, tiled=True)
    head_cast = lax.optimization_barrier(head_total.astype(jnp.bfloat16))
    totals = None
    for passage_slot in range(passage_count):
        terms = encode_backward(
            hidden[passage_slot],
            last_query[passage_slot],
            head_cast[passage_slot],
            norm_gain,
            key_full,
            value_full,
            key_first,
            key_adapter_up,
            value_first,
            value_adapter_up,
        )
        if totals is None:
            totals = terms
        else:
            totals = tuple((total_part + term_part for total_part, term_part in zip(totals, terms)))
    down_key, down_value, up_key, up_value = totals
    key_down_grad, value_down_grad = (
        lax.psum_scatter(down_key, ("batch", "fsdp"), scatter_dimension=0, tiled=True),
        lax.psum_scatter(down_value, ("batch", "fsdp"), scatter_dimension=0, tiled=True),
    )
    key_up_grad, value_up_grad = lax.psum((up_key, up_value), ("batch", "fsdp"))
    return (
        losses,
        query_embedding_gradient,
        passage_embedding_gradient,
        key_down_grad,
        value_down_grad,
        key_up_grad,
        value_up_grad,
    )


def solution(mesh):
    placed = (
        P(("batch", "fsdp"), None),
        P(("batch", "fsdp"), None),
        P(("batch", "fsdp")),
        P(("batch", "fsdp"), None, None),
        P(),
        P(("batch", "fsdp"), None),
        P("fsdp", None),
        P("fsdp", None),
        P("fsdp", None),
        P(),
        P("fsdp", None),
        P(),
        P("batch", "fsdp"),
    )
    return jax.shard_map(
        shards,
        mesh=mesh,
        in_specs=placed,
        out_specs=(
            P(("batch", "fsdp")),
            P(("batch", "fsdp"), None),
            P(("batch", "fsdp"), None),
            P(("batch", "fsdp"), None),
            P(("batch", "fsdp"), None),
            P(),
            P(),
        ),
        check_vma=False,
    )
```

profile of v0, /device:TPU:1, one launch (start us, length us, event | category | flops | bytes accessed | tf_op | source)
XLA Modules:
  0.0 1285.0 jit_solution(14057996941995493710)
XLA Ops:
  8.1 72.3 %all-gather = bf16[32,2,4096]{2,1,0:T(2,128)(2,1)S(1)} all-gather(bf16[1,2,4096]{2,1,0:T(2,128)(2,1)} %bitcast.129), channel_id=1, replica_groups=mesh['batch'=16,'fsdp'=32] {'fsdp'}, dimensions={0}, use_global_device_ids=true | all-gather | bytes 540672 | tf_op jit(solution)/shard_map/all_gather | solution.py:140
  80.6 34.7 %all-gather.1 = bf16[16,2,4096]{2,1,0:T(2,128)(2,1)S(1)} all-gather(bf16[1,2,4096]{2,1,0:T(2,128)(2,1)} %bitcast.130), channel_id=1, replica_groups=mesh['batch'=16,'fsdp'=32] {'batch'}, dimensions={0}, use_global_device_ids=true | all-gather | bytes 278528 | tf_op jit(solution)/shard_map/all_gather | solution.py:143
  115.8 58.1 %pmax.7 = f32[64]{0:T(128)S(1)} all-reduce(f32[64]{0:T(128)S(1)} %get-tuple-element.43), channel_id=1, replica_groups=mesh['batch'=16,'fsdp'=32] {'fsdp'}, use_global_device_ids=true, to_apply=%region_1.2 | all-reduce | flops 64 | bytes 512 | tf_op jit(solution)/shard_map/pmax | solution.py:149
  176.8 18.2 %all-reduce = s32[64]{0:T(128)S(1)} all-reduce(s32[64]{0:T(128)S(1)} %dynamic-update-slice), channel_id=1, replica_groups=mesh['batch'=16,'fsdp'=32] {'fsdp'}, use_global_device_ids=true, to_apply=%add | all-reduce | flops 64 | bytes 512
  195.7 62.6 %psum.28 = f32[64]{0:T(128)S(1)} all-reduce(f32[64]{0:T(128)S(1)} %get-tuple-element.9), channel_id=1, replica_groups=mesh['batch'=16,'fsdp'=32] {'fsdp'}, use_global_device_ids=true, to_apply=%region_3.4 | all-reduce | flops 64 | bytes 512 | tf_op jit(solution)/shard_map/psum | solution.py:151
  261.9 3.3 fusion.6
  265.2 60.1 %all_gather.28 = bf16[4096,64]{0,1:T(8,128)(2,1)S(1)} all-gather(bf16[128,64]{0,1:T(8,128)(2,1)S(1)} %copy-done.29), channel_id=1, replica_groups=mesh['batch'=16,'fsdp'=32] {'fsdp'}, dimensions={0}, use_global_device_ids=true | all-gather | bytes 540672 | tf_op jit(solution)/shard_map/all_gather | solution.py:172
  328.8 63.7 %all_gather.31 = bf16[4096,64]{0,1:T(8,128)(2,1)S(1)} all-gather(bf16[128,64]{0,1:T(8,128)(2,1)S(1)} %copy-done.30), channel_id=1, replica_groups=mesh['batch'=16,'fsdp'=32] {'fsdp'}, dimensions={0}, use_global_device_ids=true | all-gather | bytes 540672 | tf_op jit(solution)/shard_map/all_gather | solution.py:173
  397.1 80.7 %all_gather.29 = bf16[2048,128]{1,0:T(8,128)(2,1)S(1)} all-gather(bf16[128,128]{1,0:T(8,128)(2,1)S(1)} %copy-done.22), channel_id=1, replica_groups=mesh['batch'=16,'fsdp'=32] {'batch'}, dimensions={0}, use_global_device_ids=true | all-gather | bytes 557056 | tf_op jit(solution)/shard_map/all_gather | solution.py:182
  480.7 5.6 all-to-all-start
  487.0 13.0 %all-to-all-done = bf16[2,32,128]{2,0,1:T(2,128)(2,1)S(1)} async-done(((bf16[2,32,128]{2,0,1:T(2,128)(2,1)}), bf16[2,32,128]{2,0,1:T(2,128)(2,1)S(1)}, u32[]{:S(2)}, u32[]{:S(2)}) %all-to-all-start) | async-done | bytes 16416 | tf_op jit(solution)/shard_map/all_to_all | solution.py:180
  500.3 126.5 %all-reduce.18 = (f32[64]{0:T(128)}, bf16[64,2048]{1,0:T(8,128)(2,1)S(1)}) all-reduce(f32[64]{0:T(128)} %get-tuple-element.10, f32[64,2048]{1,0:T(8,128)S(1)} %fusion.80), channel_id=1, replica_groups=mesh['batch'=16,'fsdp'=32] {'fsdp'}, use_global_device_ids=true, to_apply=%region_5.6 | all-reduce | flops 131136 | bytes 786944 | tf_op jit(solution)/shard_map/psum | solution.py:151
  627.5 3.4 fusion.79
  633.4 4.1 fusion.71
  641.9 2.2 fusion.22
  644.3 3.6 fusion.81
  654.1 1.6 fusion.82
  655.7 2.3 fusion.21
  658.3 1.9 fusion.19
  660.2 4.6 fusion
  665.7 4.0 fusion.1
  669.7 89.0 %all-reduce.13.cloned.1.call-done = bf16[64,4096]{1,0:T(8,128)(2,1)} async-done(((bf16[64,4096]{1,0:T(8,128)(2,1)}), bf16[64,4096]{1,0:T(8,128)(2,1)}) %all-reduce.13.cloned.1.call-update) | async-done | bytes 524304
  760.8 511.4 %all-reduce.17.cloned.1.call-done = (f32[4096,64]{1,0:T(8,128)}, f32[4096,64]{1,0:T(8,128)}, f32[64,512]{1,0:T(8,128)}, f32[64,512]{1,0:T(8,128)}) async-done(((f32[4096,64]{1,0:T(8,128)}, f32[4096,64]{1,0:T(8,128)}, f32[64,512]{1,0:T(8,128)}, f32[64,512]{1,0:T(8,128)}), (f32[4096,64]{1,0:T(8,128)}, f32[4096,64]{1,0:T(8,128)}, f32[64,512]{1,0:T(8,128)}, f32[64,512]{1,0:T(8,128)})) %all-reduce.17.cloned.1.call-update) | async-done | bytes 2359312
  1274.7 1.6 copy.88
  (153 shorter events, 38.6 us)
Async XLA Ops:
  8.0 633.9 %copy-start = (bf16[64,512]{1,0:T(8,128)(2,1)S(1)}, bf16[64,512]{1,0:T(8,128)(2,1)}, u32[]{:S(2)}) copy-start(bf16[64,512]{1,0:T(8,128)(2,1)} %param.24) | copy-start | bytes 196612
  8.0 253.9 %copy-start.36 = (bf16[4096]{0:T(1024)(128)(2,1)S(1)}, bf16[4096]{0:T(1024)(128)(2,1)}, u32[]{:S(2)}) copy-start(bf16[4096]{0:T(1024)(128)(2,1)} %param.17) | copy-start | bytes 24580
  8.0 471.1 %all-reduce.15.cloned.1.call-start = ((), (), s32[]{:S(2)}) async-start(), calls=%async_computation.4 | async-start | bytes 1048576
  115.5 149.7 %copy-start.29 = (bf16[128,64]{0,1:T(8,128)(2,1)S(1)}, bf16[128,64]{0,1:T(8,128)(2,1)}, u32[]{:S(2)}) copy-start(bf16[128,64]{0,1:T(8,128)(2,1)} %param.21) | copy-start | bytes 49156
  173.9 151.3 %copy-start.34 = (f32[64]{0:T(128)}, f32[64]{0:T(128)S(1)}, u32[]{:S(2)}) copy-start(f32[64]{0:T(128)S(1)} %pmax.7) | copy-start | bytes 772
  258.3 67.0 %copy-start.37 = (f32[64]{0:T(128)}, f32[64]{0:T(128)S(1)}, u32[]{:S(2)}) copy-start(f32[64]{0:T(128)S(1)} %psum.28) | copy-start | bytes 772
  259.4 368.1 %all-gather.5.cloned.1.call-start = ((), (), s32[]{:S(2)}) async-start(), calls=%async_computation.1 | async-start | bytes 4325376 | tf_op jit(solution)/shard_map/all_gather | solution.py:170
  260.0 384.3 %all-gather.7.cloned.1.call-start = ((), (), s32[]{:S(2)}) async-start(), calls=%async_computation.2 | async-start | bytes 4325376 | tf_op jit(solution)/shard_map/all_gather | solution.py:171
  260.6 498.1 %all-reduce.13.cloned.1.call-start = ((), (), s32[]{:S(2)}) async-start(), calls=%async_computation.3 | async-start | bytes 1048576
  261.8 63.4 %copy-start.1 = (bf16[2,256,4096]{2,1,0:T(8,128)(2,1)S(1)}, bf16[2,256,4096]{2,1,0:T(8,128)(2,1)}, u32[]{:S(2)}) copy-start(bf16[2,256,4096]{2,1,0:T(8,128)(2,1)} %param.16) | copy-start | bytes 12582916
  325.3 68.6 %copy-start.31 = (f32[256]{0:T(256)}, f32[256]{0:T(256)S(1)}, u32[]{:S(2)}) copy-start(f32[256]{0:T(256)S(1)} %get-tuple-element.53) | copy-start | bytes 3076
  392.5 93.9 %copy-start.23 = (bf16[2,2048]{1,0:T(2,128)(2,1)S(1)}, bf16[2,2048]{1,0:T(2,128)(2,1)}, u32[]{:S(2)}) copy-start(bf16[2,2048]{1,0:T(2,128)(2,1)} %param.18) | copy-start | bytes 24580
  480.7 19.3 %all-to-all-start = ((bf16[2,32,128]{2,0,1:T(2,128)(2,1)}), bf16[2,32,128]{2,0,1:T(2,128)(2,1)S(1)}, u32[]{:S(2)}, u32[]{:S(2)}) async-start(bf16[2,32,128]{2,0,1:T(2,128)(2,1)} %get-tuple-element.21), calls=%async_computation | async-start | bytes 32768 | tf_op jit(solution)/shard_map/all_to_all | solution.py:180
  486.3 785.9 %all-reduce.17.cloned.1.call-start = ((), (), s32[]{:S(2)}) async-start(), calls=%async_computation.5 | async-start | bytes 8912896
  500.3 130.6 %copy-start.4 = (bf16[64,512]{1,0:T(8,128)(2,1)S(1)}, bf16[64,512]{1,0:T(8,128)(2,1)}, u32[]{:S(2)}) copy-start(bf16[64,512]{1,0:T(8,128)(2,1)} %param.22) | copy-start | bytes 196612
  644.2 5.7 copy-start.2
  644.3 5.7 copy-start.32
  658.1 6.7 copy-start.6
  658.1 6.7 copy-start.14
  658.1 7.5 copy-start.3
  658.1 7.5 copy-start.33
  665.7 94.5 %copy-start.35 = (f32[64]{0:T(128)S(1)}, f32[64]{0:T(128)}, u32[]{:S(2)}) copy-start(f32[64]{0:T(128)} %copy-done.34) | copy-start | bytes 772
  665.7 94.5 %copy-start.38 = (f32[64]{0:T(128)S(1)}, f32[64]{0:T(128)}, u32[]{:S(2)}) copy-start(f32[64]{0:T(128)} %copy-done.37) | copy-start | bytes 772
  665.7 94.5 %copy-start.39 = (f32[64]{0:T(128)S(1)}, f32[64]{0:T(128)}, u32[]{:S(2)}) copy-start(f32[64]{0:T(128)} %get-tuple-element.19) | copy-start | bytes 772
  (23 other events, 71.9 us)
Sparse Core Ops, SparseCore 0:
  259.5 180.4 all-reduce.14
  443.1 315.5 all-reduce.12
  765.1 507.0 all-reduce.16
Sparse Core Ops, SparseCore 1:
  263.0 181.3 all-gather.4
  447.3 165.3 all-gather.6
where the time goes:
time: 1290 us; the launch traced here: 1280 us
  waiting for transfers between devices  615 us (48%)
  blocking collectives  577 us (45%)
  matrix products  44.2 us (3%)
  between operations  17.8 us (1%)
  local copies, waits for them, and re-layouts  14.2 us (1%)
    unnamed x8, waiting for transfers between devices  602 us
    psum x2, blocking collectives, shards(): lax.psum((jnp.sum(exponent, axis=1), jnp.sum(similarity_scores * onehot,...  189 us
    all_gather x1, blocking collectives, shards(): output_block = lax.all_gather(out_weight, 'batch', axis=0, tiled=True)  80.7 us
    all_gather x1, blocking collectives, shards(): lax.all_gather(queries, 'fsdp', axis=0, tiled=True)  72.3 us
    all_gather x1, blocking collectives, shards(): lax.all_gather(value_down, 'fsdp', axis=0, tiled=True)  63.7 us
    all_gather x1, blocking collectives, shards(): lax.all_gather(key_down, 'fsdp', axis=0, tiled=True)  60.1 us
    pmax x1, blocking collectives, shards(): row_max = lax.pmax(jnp.max(similarity_scores, axis=1), 'fsdp')  58.1 us
    all_gather x1, blocking collectives, shards(): passage_block = lax.all_gather(passages, 'batch', axis=0, tiled=True)  34.7 us
  transfers between devices with their start and end apart: 6, of which 3 were waited for; matrix products, arithmetic and copies ran while one was open for 5% of the time, Pallas kernels for 0%

commit v1 on v0

v1 whole, which is shorter than its diff:
```python
import jax
import jax.numpy as jnp
from jax import lax
from jax.experimental import pallas as pl
from jax.experimental.pallas import tpu as pltpu
from jax.sharding import PartitionSpec as P

F32 = jnp.float32
BF16 = jnp.bfloat16
MESH = pl.DeviceIdType.MESH
HEAD = 128
SCALE = 20.0
EPSILON = 1e-06
ROTARY_BASE = 1000000.0
VMEM_BYTES = 56 * 1024 * 1024


def position():
    b = lax.axis_index("batch")
    f = lax.axis_index("fsdp")
    y = b // 4
    xlo = (b // 2) % 2
    c = b % 2
    z = f // 2
    xhi = f % 2
    return (b, f, y, xlo, c, z, xhi)


def remote(src, dst, send_sem, recv_sem, b, f):
    return pltpu.make_async_remote_copy(
        src_ref=src,
        dst_ref=dst,
        send_sem=send_sem,
        recv_sem=recv_sem,
        device_id=(b, f),
        device_id_type=MESH,
    )


def loop(lo, hi, body):
    def step(i, carry):
        body(i)
        return carry

    lax.fori_loop(lo, hi, step, 0)


def iota(shape, dim):
    return lax.broadcasted_iota(jnp.int32, shape, dim)


def dot(a, b, ca=1, cb=0, precision=None):
    return lax.dot_general(
        a, b, (((ca,), (cb,)), ((), ())), preferred_element_type=F32, precision=precision
    )


def gather_kernel(
    q_in,
    p_in,
    wo_in,
    wh_in,
    loss_out,
    qg_out,
    pg_out,
    head_out,
    wf,
    qs,
    ps,
    ws,
    wg,
    qwg,
    st,
    pgs,
    pgr,
    hps,
    hpr,
    qgs,
    qgx,
    qgr,
    q_send,
    q_recv,
    qx_send,
    qx_recv,
    w_send,
    w_recv,
    p_send,
    p_recv,
    w1_send,
    w1_recv,
    w2_send,
    w2_recv,
    w3_sem,
    qw_send,
    qw_recv,
    qwx_send,
    qwx_recv,
    st_send,
    st_recv,
    pg_send,
    pg_recv,
    hp_send,
    hp_recv,
    qg_send,
    qg_recv,
    qgx_sem,
    ax_send,
    ax_recv,
    ay_send,
    ay_recv,
    by_send,
    by_recv,
    bx_send,
    bx_recv,
    wx_send,
    wx_recv,
    loc_sem,
):
    b, f, y, xlo, c, z, xhi = position()
    pi = (b // 2) * 2 + xhi
    sib = b + 1 - 2 * c
    line = c * 16 + z

    def plane_dev(t):
        return ((t // 2) * 2 + c, z * 2 + t % 2)

    def line_dev(s):
        return ((b // 2) * 2 + s // 16, (s % 16) * 2 + xhi)

    barrier = pltpu.get_barrier_semaphore()

    def greet_plane(i):
        tb, tf = plane_dev((pi + i) % 16)
        pl.semaphore_signal(barrier, inc=1, device_id=(tb, tf), device_id_type=MESH)

    def greet_line(i):
        tb, tf = line_dev((line + i) % 32)
        pl.semaphore_signal(barrier, inc=1, device_id=(tb, tf), device_id_type=MESH)

    loop(1, 16, greet_plane)
    loop(1, 32, greet_line)
    qs[c, z] = q_in[...]
    ps[pi] = p_in[...]
    wf[c, z, xhi, y, xlo] = wh_in[pl.ds((y * 2 + xlo) * 16, 16), :]
    pl.semaphore_wait(barrier, 46)

    right = ((z + 1) % 16) * 2 + xhi
    left = ((z + 15) % 16) * 2 + xhi

    def q_hop(src, way, to):
        return remote(qs.at[c, src], qs.at[c, src], q_send.at[way, src], q_recv.at[src], b, to)

    def w_hop(src, way, to):
        piece = wf.at[c, src, xhi, y, xlo]
        return remote(piece, piece, w_send.at[way, src], w_recv.at[src], b, to)

    def q_cross(src):
        return remote(qs.at[c, src], qs.at[c, src], qx_send.at[src], qx_recv.at[src], sib, f)

    q_hop(z, 0, right).start()
    q_hop(z, 1, left).start()
    q_cross(z).start()
    w_hop(z, 0, right).start()
    w_hop(z, 1, left).start()

    def wo_move(zp):
        return remote(
            wo_in.at[pl.ds(zp * 16, 16), :],
            ws.at[z % 2, z // 2],
            w1_send.at[zp],
            w1_recv.at[z],
            (b // 2) * 2 + xlo,
            (2 * zp + c) * 2 + xhi,
        )

    def wo_start(zp):
        here = jnp.logical_and(c == xlo, 2 * zp + c == z)

        @pl.when(jnp.logical_not(here))
        def _():
            wo_move(zp).start()

        @pl.when(here)
        def _():
            ws[z % 2, z // 2] = wo_in[pl.ds(zp * 16, 16), :]

    loop(0, 8, wo_start)

    def p_move(i):
        t = (pi + i) % 16
        tb, tf = plane_dev(t)
        return remote(ps.at[pi], ps.at[pi], p_send.at[t], p_recv.at[pi], tb, tf)

    loop(1, 16, lambda i: p_move(i).start())

    def ring(k):
        a = (z + 16 - k) % 16
        q_hop(a, 0, right).wait_recv()

        @pl.when(k < 8)
        def _():
            q_hop(a, 0, right).start()

        q_cross(a).start()
        w_hop(a, 0, right).wait_recv()

        @pl.when(k < 8)
        def _():
            w_hop(a, 0, right).start()

        @pl.when(k < 8)
        def _():
            e = (z + k) % 16
            q_hop(e, 1, left).wait_recv()

            @pl.when(k < 7)
            def _():
                q_hop(e, 1, left).start()

            q_cross(e).start()
            w_hop(e, 1, left).wait_recv()

            @pl.when(k < 7)
            def _():
                w_hop(e, 1, left).start()

    loop(1, 4, ring)

    mine = c == xlo

    def wo_slot(t, yy):
        return wg.at[:, t, :, pl.ds((c * 4 + yy) * 16, 16), :]

    def wo_spread(i):
        t = (pi + i) % 16
        tb, tf = plane_dev(t)
        return remote(ws, wo_slot(xhi, y), w2_send.at[t], w2_recv.at[y * 2 + xhi], tb, tf)

    @pl.when(mine)
    def _():
        def wait_one(zz):
            @pl.when(jnp.logical_not(jnp.logical_and(z % 2 == c, zz == z)))
            def _():
                remote(
                    wo_in.at[pl.ds(0, 16), :],
                    ws.at[zz % 2, zz // 2],
                    w1_send.at[0],
                    w1_recv.at[zz],
                    sib,
                    f,
                ).wait_recv()

        loop(0, 16, wait_one)
        loop(1, 16, lambda i: wo_spread(i).start())
        wg[:, xhi, :, pl.ds((c * 4 + y) * 16, 16), :] = ws[...]

    loop(4, 9, ring)

    lo_z, hi_z = pl.ds(0, 8), pl.ds(8, 8)

    def x_of(i):
        return (xhi * 2 + xlo + i) % 4

    def x_dev(i):
        x = x_of(i)
        return (y * 4 + (x % 2) * 2 + c, z * 2 + x // 2)

    def y_dev(i):
        return (((y + i) % 4) * 4 + xlo * 2 + c, f)

    def ax_move(i):
        part = wf.at[c, lo_z, xhi, y, xlo]
        tb, tf = x_dev(i)
        return remote(part, part, ax_send.at[i], ax_recv.at[4 - i], tb, tf)

    def by_move(i):
        part = wf.at[c, hi_z, xhi, y, xlo]
        tb, tf = y_dev(i)
        return remote(part, part, by_send.at[i], by_recv.at[4 - i], tb, tf)

    loop(1, 4, lambda i: ax_move(i).start())
    loop(1, 4, lambda i: by_move(i).start())

    def p_wait(i):
        t = (pi + i) % 16
        remote(ps.at[t], ps.at[t], p_send.at[t], p_recv.at[t], sib, f).wait_recv()

    loop(1, 16, p_wait)

    def qx_wait(zz):
        slot = qs.at[1 - c, zz]
        remote(slot, slot, qx_send.at[zz], qx_recv.at[zz], sib, f).wait_recv()

    loop(0, 16, qx_wait)

    q_all = qs[...].reshape(512, 640)
    q_rows = q_all[:, :512]
    p_rows = ps[...].reshape(256, 512)
    wide = dot(p_rows, q_rows, 1, 1).reshape(32, 8, 512)
    same = iota((32, 8, 512), 1) == iota((32, 8, 512), 2) % 8
    folded = jnp.sum(jnp.where(same, wide, 0.0), axis=1)
    fold = (iota((512, 64), 0) // 8 == iota((512, 64), 1)).astype(F32)
    scores = SCALE * dot(folded, fold, precision=lax.Precision.HIGHEST)
    marks = dot(q_all[:, 512:], fold.astype(BF16), 0, 0)
    target = marks[0:1] * 32.0 + marks[1:2]
    pid = iota((32, 64), 0)
    ptile = pid // 2
    ids = (((ptile // 2) * 2 + c) * 32 + z * 2 + ptile % 2) * 2 + pid % 2
    hit = (ids.astype(F32) == target).astype(F32)
    top = jnp.max(scores, axis=0, keepdims=True)
    local = top + jnp.log(jnp.sum(jnp.exp(scores - top), axis=0, keepdims=True))
    st[line] = jnp.zeros((4, 128), F32)
    st[line, 0:1, 0:64] = local
    st[line, 1:2, 0:64] = jnp.sum(scores * hit, axis=0, keepdims=True)

    def st_move(i):
        s = (line + i) % 32
        tb, tf = line_dev(s)
        return remote(st.at[line], st.at[line], st_send.at[s], st_recv.at[line], tb, tf)

    loop(1, 32, lambda i: st_move(i).start())

    half = wg.at[:, :, :, pl.ds(c * 64, 64), :]
    other = wg.at[:, :, :, pl.ds((1 - c) * 64, 64), :]

    def wo_wait(s):
        @pl.when(jnp.logical_not(jnp.logical_and(mine, s == y * 2 + xhi)))
        def _():
            slot = wo_slot(s % 2, s // 2)
            remote(ws, slot, w2_send.at[0], w2_recv.at[s], sib, f).wait_recv()

    loop(0, 8, wo_wait)
    cross = remote(half, half, w3_sem.at[0], w3_sem.at[1], sib, f)
    cross.start()
    remote(other, other, w3_sem.at[0], w3_sem.at[1], sib, f).wait_recv()
    q_half = qs[c].reshape(256, 640)
    prod = jnp.zeros((256, 1024), F32)
    for a in range(4):
        prod += dot(
            q_half[:, a * 128 : (a + 1) * 128], wg[a // 2, a % 2].reshape(1024, 128), 1, 1
        )
    qw = jnp.zeros((256, 128), F32)
    chunk = iota((256, 128), 0) % 8
    for a in range(8):
        qw += jnp.where(chunk == a, prod[:, a * 128 : (a + 1) * 128], 0.0)
    qwg[z, c] = jnp.sum(qw.reshape(32, 8, 128), axis=1).astype(BF16)

    def qw_move(i):
        zz = (z + i) % 16
        return remote(
            qwg.at[z, c], qwg.at[z, c], qw_send.at[zz], qw_recv.at[z], b, zz * 2 + xhi
        )

    def qw_cross(zz):
        return remote(qwg.at[zz, c], qwg.at[zz, c], qwx_send.at[zz], qwx_recv.at[zz], sib, f)

    loop(1, 16, lambda i: qw_move(i).start())
    qw_cross(z).start()

    def ax_wait(i):
        x = x_of(i)
        part = wf.at[c, lo_z, x // 2, y, x % 2]
        remote(part, part, ax_send.at[i], ax_recv.at[i], sib, f).wait_recv()

    def by_wait(i):
        part = wf.at[c, hi_z, xhi, (y + i) % 4, xlo]
        remote(part, part, by_send.at[i], by_recv.at[i], sib, f).wait_recv()

    def ay_move(i):
        part = wf.at[c, lo_z, :, y]
        tb, tf = y_dev(i)
        return remote(part, part, ay_send.at[i], ay_recv.at[4 - i], tb, tf)

    def bx_move(i):
        part = wf.at[c, hi_z, xhi, :, xlo]
        tb, tf = x_dev(i)
        return remote(part, part, bx_send.at[i], bx_recv.at[4 - i], tb, tf)

    loop(1, 4, ax_wait)
    loop(1, 4, lambda i: ay_move(i).start())
    loop(1, 4, by_wait)
    loop(1, 4, lambda i: bx_move(i).start())

    def wx_a(yy, n):
        part = wf.at[c, lo_z, :, yy]
        return remote(part, part, wx_send.at[n], wx_recv.at[n], sib, f)

    def wx_b(x, n):
        part = wf.at[c, hi_z, x // 2, :, x % 2]
        return remote(part, part, wx_send.at[n + 4], wx_recv.at[n + 4], sib, f)

    wx_a(y, 0).start()
    wx_b(xhi * 2 + xlo, 0).start()

    def st_wait(i):
        s = (line + i) % 32
        remote(st.at[s], st.at[s], st_send.at[s], st_recv.at[s], sib, f).wait_recv()

    loop(1, 32, st_wait)
    stats = st[...]
    peak = jnp.max(stats, axis=0)
    total = peak + jnp.log(jnp.sum(jnp.exp(stats - peak[None]), axis=0))
    picked = jnp.sum(stats, axis=0)
    lse = total[0:1, :64]
    loss_out[...] = jnp.zeros_like(loss_out)
    loss_out[0:1, 0:64] = lse - picked[1:2, :64]
    weights = (jnp.exp(scores - lse) - hit).astype(BF16)

    rows8 = (iota((256, 32), 0) // 8 == iota((256, 32), 1)).astype(BF16)
    cols8 = (iota((64, 512), 1) // 8 == iota((64, 512), 0)).astype(BF16)
    spread = dot(dot(rows8, weights).astype(BF16), cols8)
    diag = iota((256, 512), 0) % 8 == iota((256, 512), 1) % 8
    spread = jnp.where(diag, spread, 0.0).astype(BF16)
    pgs[...] = (SCALE * dot(spread, q_rows)).astype(BF16).reshape(16, 16, 512)

    def pg_move(i):
        t = (pi + i) % 16
        tb, tf = plane_dev(t)
        return remote(pgs.at[t], pgr.at[pi], pg_send.at[t], pg_recv.at[pi], tb, tf)

    def hp_move(i):
        t = (pi + i) % 16
        tb, tf = plane_dev(t)
        return remote(hps.at[t], hpr.at[pi], hp_send.at[t], hp_recv.at[pi], tb, tf)

    def qw_wait(i):
        zz = (z + i) % 16
        remote(qwg.at[zz, c], qwg.at[zz, c], qw_send.at[zz], qw_recv.at[zz], sib, f).wait_recv()
        qw_cross(zz).start()

    loop(1, 16, qw_wait)

    def qwx_wait(zz):
        slot = qwg.at[zz, 1 - c]
        remote(slot, slot, qwx_send.at[zz], qwx_recv.at[zz], sib, f).wait_recv()

    loop(0, 16, qwx_wait)
    rows16 = (iota((512, 32), 0) // 16 == iota((512, 32), 1)).astype(BF16)
    cols64 = (iota((64, 1024), 1) % 64 == iota((64, 1024), 0)).astype(BF16)
    tall = dot(dot(rows16, weights).astype(BF16), cols64)
    diag = iota((512, 1024), 0) % 16 == iota((512, 1024), 1) // 64
    tall = jnp.where(diag, tall, 0.0).astype(BF16)
    hps[...] = (SCALE * dot(tall, qwg[...].reshape(1024, 128))).astype(BF16).reshape(16, 32, 128)
    loop(1, 16, lambda i: hp_move(i).start())
    loop(1, 16, lambda i: pg_move(i).start())
    hpr[pi] = hps[pi]
    pgr[pi] = pgs[pi]

    qgs[...] = (SCALE * dot(spread, p_rows, 0, 0)).astype(BF16).reshape(2, 16, 16, 512)
    swap = remote(qgs.at[1 - c], qgx, qgx_sem.at[0], qgx_sem.at[1], sib, f)
    swap.start()
    swap.wait_recv()
    qgs[c] = (qgs[c].astype(F32) + qgx[...].astype(F32)).astype(BF16)

    def qg_move(i):
        zz = (z + i) % 16
        return remote(qgs.at[c, zz], qgr.at[z], qg_send.at[zz], qg_recv.at[z], b, zz * 2 + xhi)

    loop(1, 16, lambda i: qg_move(i).start())
    qgr[z] = qgs[c, z]

    def hp_wait(i):
        t = (pi + i) % 16
        remote(hps.at[t], hpr.at[t], hp_send.at[t], hp_recv.at[t], sib, f).wait_recv()

    def pg_wait(i):
        t = (pi + i) % 16
        remote(pgs.at[t], pgr.at[t], pg_send.at[t], pg_recv.at[t], sib, f).wait_recv()

    def qg_wait(i):
        t = (z + i) % 16
        remote(qgs.at[c, t], qgr.at[t], qg_send.at[t], qg_recv.at[t], sib, f).wait_recv()

    loop(1, 16, hp_wait)
    head_out[...] = jnp.sum(hpr[...].astype(F32), axis=0)
    loop(1, 16, pg_wait)
    pg_out[...] = jnp.sum(pgr[...].astype(F32), axis=0)

    def ay_wait(i):
        part = wf.at[c, lo_z, :, (y + i) % 4]
        remote(part, part, ay_send.at[i], ay_recv.at[i], sib, f).wait_recv()
        wx_a((y + i) % 4, i).start()

    def bx_wait(i):
        x = x_of(i)
        part = wf.at[c, hi_z, x // 2, :, x % 2]
        remote(part, part, bx_send.at[i], bx_recv.at[i], sib, f).wait_recv()
        wx_b(x, i).start()

    loop(1, 4, ay_wait)
    loop(1, 4, bx_wait)
    loop(1, 16, qg_wait)
    qg_out[...] = jnp.sum(qgr[...].astype(F32), axis=0)

    def wx_wait(n):
        x = x_of(n)
        part = wf.at[1 - c, lo_z, :, (y + n) % 4]
        remote(part, part, wx_send.at[n], wx_recv.at[n], sib, f).wait_recv()
        part = wf.at[1 - c, hi_z, x // 2, :, x % 2]
        remote(part, part, wx_send.at[n + 4], wx_recv.at[n + 4], sib, f).wait_recv()

    loop(0, 4, wx_wait)

    def ring_sent(k):
        a = (z + 16 - k) % 16
        q_hop(a, 0, right).wait_send()
        w_hop(a, 0, right).wait_send()

        @pl.when(k < 7)
        def _():
            e = (z + k) % 16
            q_hop(e, 1, left).wait_send()
            w_hop(e, 1, left).wait_send()

    loop(0, 8, ring_sent)
    loop(0, 16, lambda zz: q_cross(zz).wait_send())

    def wo_sent(zp):
        @pl.when(jnp.logical_not(jnp.logical_and(mine, 2 * zp + c == z)))
        def _():
            wo_move(zp).wait_send()

    loop(0, 8, wo_sent)

    @pl.when(mine)
    def _():
        loop(1, 16, lambda i: wo_spread(i).wait_send())

    cross.wait_send()
    loop(1, 16, lambda i: p_move(i).wait_send())
    loop(1, 32, lambda i: st_move(i).wait_send())
    loop(1, 16, lambda i: qw_move(i).wait_send())
    loop(0, 16, lambda zz: qw_cross(zz).wait_send())
    loop(1, 16, lambda i: pg_move(i).wait_send())
    loop(1, 16, lambda i: hp_move(i).wait_send())
    swap.wait_send()
    loop(1, 16, lambda i: qg_move(i).wait_send())
    loop(1, 4, lambda i: ax_move(i).wait_send())
    loop(1, 4, lambda i: by_move(i).wait_send())
    loop(1, 4, lambda i: ay_move(i).wait_send())
    loop(1, 4, lambda i: bx_move(i).wait_send())

    def wx_sent(n):
        wx_a((y + n) % 4, n).wait_send()
        wx_b(x_of(n), n).wait_send()

    loop(0, 4, wx_sent)


def gather_call(q, p, wo, wh):
    dma = pltpu.SemaphoreType.DMA
    vm = pl.BlockSpec(memory_space=pltpu.VMEM)
    return pl.pallas_call(
        gather_kernel,
        out_shape=(
            jax.ShapeDtypeStruct((8, 128), F32),
            jax.ShapeDtypeStruct((16, 512), F32),
            jax.ShapeDtypeStruct((16, 512), F32),
            jax.ShapeDtypeStruct((32, 128), F32),
            jax.ShapeDtypeStruct((2, 16, 2, 4, 2, 16, 640), BF16),
        ),
        in_specs=[vm] * 4,
        out_specs=(vm,) * 5,
        scratch_shapes=[
            pltpu.VMEM((2, 16, 16, 640), BF16),
            pltpu.VMEM((16, 16, 512), BF16),
            pltpu.VMEM((2, 8, 16, 128), BF16),
            pltpu.VMEM((2, 2, 8, 128, 128), BF16),
            pltpu.VMEM((16, 2, 32, 128), BF16),
            pltpu.VMEM((32, 4, 128), F32),
            pltpu.VMEM((16, 16, 512), BF16),
            pltpu.VMEM((16, 16, 512), BF16),
            pltpu.VMEM((16, 32, 128), BF16),
            pltpu.VMEM((16, 32, 128), BF16),
            pltpu.VMEM((2, 16, 16, 512), BF16),
            pltpu.VMEM((16, 16, 512), BF16),
            pltpu.VMEM((16, 16, 512), BF16),
            dma((2, 16)),
            dma((16,)),
            dma((16,)),
            dma((16,)),
            dma((2, 16)),
            dma((16,)),
            dma((16,)),
            dma((16,)),
            dma((8,)),
            dma((16,)),
            dma((16,)),
            dma((8,)),
            dma((2,)),
            dma((16,)),
            dma((16,)),
            dma((16,)),
            dma((16,)),
            dma((32,)),
            dma((32,)),
            dma((16,)),
            dma((16,)),
            dma((16,)),
            dma((16,)),
            dma((16,)),
            dma((16,)),
            dma((2,)),
            dma((4,)),
            dma((4,)),
            dma((4,)),
            dma((4,)),
            dma((4,)),
            dma((4,)),
            dma((4,)),
            dma((4,)),
            dma((8,)),
            dma((8,)),
            dma((1,)),
        ],
        compiler_params=pltpu.CompilerParams(
            collective_id=0, has_side_effects=True, vmem_limit_bytes=VMEM_BYTES
        ),
    )(q, p, wo, wh)


def reduce_kernel(
    d_in,
    u_in,
    d_out,
    uk_out,
    uv_out,
    d1,
    r1,
    d2,
    r2,
    d3,
    u1,
    v1,
    u2,
    v3,
    u3,
    u4,
    u5,
    one_send,
    one_recv,
    d2_send,
    d2_recv,
    d3_send,
    d3_recv,
    u2_send,
    u2_recv,
    u3_send,
    u3_recv,
    u4_send,
    u4_recv,
):
    b, f, y, xlo, c, z, xhi = position()
    pi = (b // 2) * 2 + xhi
    sib = b + 1 - 2 * c

    def plane_dev(t):
        return ((t // 2) * 2 + c, z * 2 + t % 2)

    barrier = pltpu.get_barrier_semaphore()

    def greet_plane(i):
        q = ((b // 2) + i) % 8
        pl.semaphore_signal(
            barrier, inc=1, device_id=(q * 2 + c, z * 2), device_id_type=MESH
        )
        pl.semaphore_signal(
            barrier, inc=1, device_id=(q * 2 + c, z * 2 + 1), device_id_type=MESH
        )

    def greet_line(i):
        pl.semaphore_signal(barrier, inc=1, device_id=(b, (f + i) % 32), device_id_type=MESH)

    pl.semaphore_signal(barrier, inc=1, device_id=(sib, f), device_id_type=MESH)
    loop(1, 8, greet_plane)
    loop(1, 32, greet_line)
    pl.semaphore_wait(barrier, 46)

    u_swap = remote(u_in.at[1 - c], u1, one_send.at[0], one_recv.at[0], sib, f)
    d_swap = remote(d_in.at[:, 1 - c], d1, one_send.at[1], one_recv.at[1], sib, f)
    u_swap.start()
    d_swap.start()
    u_swap.wait_recv()
    v1[...] = (u_in[c].astype(F32) + u1[...].astype(F32)).astype(BF16)

    def u2_move(i):
        t = (pi + i) % 16
        tb, tf = plane_dev(t)
        return remote(v1.at[t], u2.at[pi], u2_send.at[t], u2_recv.at[pi], tb, tf)

    def d2_move(i):
        t = (pi + i) % 16
        tb, tf = plane_dev(t)
        return remote(r1.at[t], d2.at[pi], d2_send.at[t], d2_recv.at[pi], tb, tf)

    loop(1, 16, lambda i: u2_move(i).start())
    u2[pi] = v1[pi]
    d_swap.wait_recv()
    r1[...] = (
        (d_in[:, c].astype(F32) + d1[...].astype(F32)).astype(BF16).reshape(16, 128, 128)
    )
    loop(1, 16, lambda i: d2_move(i).start())
    d2[pi] = r1[pi]

    def u2_wait(i):
        t = (pi + i) % 16
        remote(v1.at[t], u2.at[t], u2_send.at[t], u2_recv.at[t], sib, f).wait_recv()

    loop(1, 16, u2_wait)
    v3[...] = jnp.sum(u2[...].astype(F32), axis=0)
    u3[z] = v3[...]

    def u3_move(i):
        zz = (z + i) % 16
        return remote(v3, u3.at[z], u3_send.at[zz], u3_recv.at[z], b, zz * 2 + xhi)

    loop(1, 16, lambda i: u3_move(i).start())

    def d2_wait(i):
        t = (pi + i) % 16
        remote(r1.at[t], d2.at[t], d2_send.at[t], d2_recv.at[t], sib, f).wait_recv()

    loop(1, 16, d2_wait)
    r2[...] = jnp.sum(d2[...].astype(F32), axis=0).reshape(16, 8, 128)

    def d3_move(k):
        return remote(
            r2.at[k], d3.at[z], d3_send.at[k], d3_recv.at[z], b, (8 * xhi + k // 2) * 2 + k % 2
        )

    own = jnp.logical_and(z // 8 == xhi, True)

    def d3_self(k):
        return (8 * xhi + k // 2) * 2 + k % 2 == f

    def d3_start(k):
        @pl.when(jnp.logical_not(d3_self(k)))
        def _():
            d3_move(k).start()

        @pl.when(d3_self(k))
        def _():
            d3[z] = r2[k]

    loop(0, 16, d3_start)

    def u3_wait(i):
        t = (z + i) % 16
        remote(v3, u3.at[t], u3_send.at[t], u3_recv.at[t], sib, f).wait_recv()

    loop(1, 16, u3_wait)
    u4[pi] = jnp.sum(u3[...], axis=0)

    def u4_move(i):
        t = (pi + i) % 16
        tb, tf = plane_dev(t)
        return remote(u4.at[pi], u4.at[pi], u4_send.at[t], u4_recv.at[pi], tb, tf)

    loop(1, 16, lambda i: u4_move(i).start())

    def d3_wait(zz):
        @pl.when(jnp.logical_not(jnp.logical_and(own, zz == z)))
        def _():
            remote(r2.at[0], d3.at[zz], d3_send.at[0], d3_recv.at[zz], sib, f).wait_recv()

    loop(0, 16, d3_wait)
    d_out[...] = jnp.sum(d3[...], axis=0)

    def u4_wait(i):
        t = (pi + i) % 16
        remote(u4.at[t], u4.at[t], u4_send.at[t], u4_recv.at[t], sib, f).wait_recv()

    loop(1, 16, u4_wait)
    back = remote(u4, u5, one_send.at[2], one_recv.at[2], sib, f)
    back.start()
    back.wait_recv()

    def put(out, src):
        full = src[...].reshape(256, 128)
        for k in range(4):
            out[:, k * 128 : (k + 1) * 128] = full[k * 64 : (k + 1) * 64]

    @pl.when(c == 0)
    def _():
        put(uk_out, u4)
        put(uv_out, u5)

    @pl.when(c == 1)
    def _():
        put(uk_out, u5)
        put(uv_out, u4)

    u_swap.wait_send()
    d_swap.wait_send()
    back.wait_send()
    loop(1, 16, lambda i: u2_move(i).wait_send())
    loop(1, 16, lambda i: d2_move(i).wait_send())
    loop(1, 16, lambda i: u3_move(i).wait_send())
    loop(1, 16, lambda i: u4_move(i).wait_send())

    def d3_sent(k):
        @pl.when(jnp.logical_not(d3_self(k)))
        def _():
            d3_move(k).wait_send()

    loop(0, 16, d3_sent)


def reduce_call(d, u):
    dma = pltpu.SemaphoreType.DMA
    vm = pl.BlockSpec(memory_space=pltpu.VMEM)
    return pl.pallas_call(
        reduce_kernel,
        out_shape=(
            jax.ShapeDtypeStruct((8, 128), F32),
            jax.ShapeDtypeStruct((64, 512), F32),
            jax.ShapeDtypeStruct((64, 512), F32),
        ),
        in_specs=[vm] * 2,
        out_specs=(vm,) * 3,
        scratch_shapes=[
            pltpu.VMEM((8, 256, 128), BF16),
            pltpu.VMEM((16, 128, 128), BF16),
            pltpu.VMEM((16, 128, 128), BF16),
            pltpu.VMEM((16, 8, 128), F32),
            pltpu.VMEM((16, 8, 128), F32),
            pltpu.VMEM((16, 16, 128), BF16),
            pltpu.VMEM((16, 16, 128), BF16),
            pltpu.VMEM((16, 16, 128), BF16),
            pltpu.VMEM((16, 128), F32),
            pltpu.VMEM((16, 16, 128), F32),
            pltpu.VMEM((16, 16, 128), F32),
            pltpu.VMEM((16, 16, 128), F32),
            dma((3,)),
            dma((3,)),
        ]
        + [dma((16,))] * 10,
        compiler_params=pltpu.CompilerParams(
            collective_id=1, has_side_effects=True, vmem_limit_bytes=VMEM_BYTES
        ),
    )(d, u)


def rotary_tables(length):
    half = HEAD // 2
    place = jnp.arange(length, dtype=F32)
    frequency = ROTARY_BASE ** (-(jnp.arange(half, dtype=F32) * 2.0 / HEAD))
    angles = place[:, None] * frequency[None, :]
    return (jnp.cos(angles)[:, None, :], jnp.sin(angles)[:, None, :])


def encode_backward(tokens, query, grad, gain, weights, key_up, value_up):
    count, length, width = tokens.shape
    groups = 4
    rows = count * length
    wide = tokens.astype(F32).reshape(rows, width)
    normed = (
        wide
        * lax.rsqrt(jnp.mean(wide * wide, axis=-1, keepdims=True) + EPSILON)
        * gain.astype(F32)
    ).astype(BF16)
    key_all = jnp.dot(normed, weights[0], preferred_element_type=F32)
    value_all = jnp.dot(normed, weights[1], preferred_element_type=F32)
    low_key = key_all[:, 512:576].astype(BF16)
    low_value = value_all[:, 512:576].astype(BF16)
    keys = key_all[:, :512] + 2.0 * jnp.dot(low_key, key_up, preferred_element_type=F32)
    values = (
        value_all[:, :512] + 2.0 * jnp.dot(low_value, value_up, preferred_element_type=F32)
    ).astype(BF16)
    keys = keys.reshape(count, length, groups, HEAD)
    cosine, sine = rotary_tables(length)
    lead, trail = keys[..., : HEAD // 2], keys[..., HEAD // 2 :]
    keys = jnp.concatenate(
        [lead * cosine - trail * sine, trail * cosine + lead * sine], axis=-1
    ).astype(BF16)
    values = values.reshape(count, length, groups, HEAD)
    q = query.reshape(count, groups, 4, HEAD)
    g = grad.reshape(count, groups, 4, HEAD)
    scores = jnp.einsum("pgjd,ptgd->pgjt", q, keys, preferred_element_type=F32) * HEAD ** (-0.5)
    attention = jax.nn.softmax(scores, axis=-1)
    prob = jnp.einsum("pgjd,ptgd->pgjt", g, values, preferred_element_type=F32)
    expected = jnp.sum(attention * prob, axis=-1, keepdims=True)
    score_grad = attention * (prob - expected)
    value_grad = jnp.einsum(
        "pgjt,pgjd->ptgd", attention.astype(BF16), g, preferred_element_type=F32
    )
    rotated = jnp.einsum(
        "pgjt,pgjd->ptgd", score_grad.astype(BF16), q, preferred_element_type=F32
    ) * HEAD ** (-0.5)
    lead, trail = rotated[..., : HEAD // 2], rotated[..., HEAD // 2 :]
    key_grad = jnp.concatenate(
        [lead * cosine + trail * sine, trail * cosine - lead * sine], axis=-1
    )
    key_cast = key_grad.reshape(rows, 512).astype(BF16)
    value_cast = value_grad.reshape(rows, 512).astype(BF16)
    up = [
        2.0 * dot(low, cast, 0, 0) for low, cast in ((low_key, key_cast), (low_value, value_cast))
    ]
    back = jnp.concatenate(
        [dot(key_cast, key_up, 1, 1), dot(value_cast, value_up, 1, 1)], axis=1
    ).astype(BF16)
    down = 2.0 * dot(normed, back, 0, 0)
    return (down, up[0], up[1])


def shards(
    queries,
    passages,
    positives,
    hidden,
    norm_gain,
    last_query,
    frozen_key_weight,
    frozen_value_weight,
    key_down,
    key_adapter_up,
    value_down,
    value_adapter_up,
    out_weight,
):
    b = lax.axis_index("batch")
    c = b % 2
    z = lax.axis_index("fsdp") // 2
    first = (jnp.arange(16) % 8 == 0)[:, None]
    spot = jnp.repeat(positives, 8)[:, None]
    lane = jnp.arange(128)[None, :]
    marks = jnp.where(lane == 0, spot // 32, jnp.where(lane == 1, spot % 32, 0))
    marks = jnp.where(first, marks, 0).astype(BF16)
    q_slab = jnp.concatenate([queries.reshape(16, 512), marks], axis=1)
    p_slab = passages.reshape(16, 512)
    pad = jnp.zeros((128, 64), BF16)
    mine = jnp.where(
        c == 0,
        jnp.concatenate([frozen_key_weight, key_down, pad], axis=1),
        jnp.concatenate([frozen_value_weight, value_down, pad], axis=1),
    )
    loss, q_grad, p_grad, head, full = gather_call(q_slab, p_slab, out_weight, mine)
    losses = lax.dynamic_slice(loss[0], ((c * 16 + z) * 2,), (2,))
    head = head.reshape(2, 8, 2, 2, 4, 16).transpose(0, 4, 3, 2, 1, 5).reshape(2, 2048)
    head = head.astype(BF16)
    down, up_key, up_value = encode_backward(
        hidden,
        last_query,
        head,
        norm_gain,
        full.reshape(2, 4096, 640),
        key_adapter_up,
        value_adapter_up,
    )
    up = jnp.stack([up_key, up_value]).reshape(2, 64, 4, 128).transpose(0, 2, 1, 3)
    grads, up_key, up_value = reduce_call(
        down.astype(BF16).reshape(8, 2, 256, 128), up.astype(BF16).reshape(2, 16, 16, 128)
    )
    return (
        losses,
        q_grad.reshape(2, 4096),
        p_grad.reshape(2, 4096),
        grads[:, :64],
        grads[:, 64:],
        up_key,
        up_value,
    )


def solution(mesh):
    rows = P(("batch", "fsdp"), None)
    placed = (
        rows,
        rows,
        P(("batch", "fsdp")),
        P(("batch", "fsdp"), None, None),
        P(),
        rows,
        P("fsdp", None),
        P("fsdp", None),
        P("fsdp", None),
        P(),
        P("fsdp", None),
        P(),
        P("batch", "fsdp"),
    )
    return jax.shard_map(
        shards,
        mesh=mesh,
        in_specs=placed,
        out_specs=(P(("batch", "fsdp")), rows, rows, rows, rows, P(), P()),
        check_vma=False,
    )
```

time: 1290 us -> 195 us (0.15)
  waiting for transfers between devices: 615 us -> 0 us
  blocking collectives: 577 us -> 0 us
  Pallas kernels: 0 us -> 135 us
  matrix products: 44.2 us -> 18.7 us
  between operations: 17.8 us -> 1 us
    unnamed x8 -> x0, waiting for transfers between devices: 602 us -> none
    all_gather x5 -> x0, blocking collectives: 312 us -> none  [the longest x1 80.7 us: shards(): output_block = lax.all_gather(out_weight, 'batch', axis=0, tiled=True)]
    psum x2 -> x0, blocking collectives: 189 us -> none  [shards(): lax.psum((jnp.sum(exponent, axis=1), jnp.sum(similarity_scores * onehot,...]
    pallas_call x0 -> x2, Pallas kernels: none -> 135 us  [the longest x1 100 us: gather_call(): pl.pallas_call(gather_kernel, out_shape=(jax.ShapeDtypeStruct((8, 128), F...]
    pmax x1 -> x0, blocking collectives: 58.1 us -> none  [shards(): row_max = lax.pmax(jnp.max(similarity_scores, axis=1), 'fsdp')]
    dot_general x32 -> x12, matrix products: 44.2 us -> 18.1 us  [the longest x1 7.05 us: encode_backward(): value_all = jnp.dot(normed, weights[1], preferred_element_type=F32)]
    unnamed x1 -> x0, blocking collectives: 18.2 us -> none
    all_to_all x1 -> x0, waiting for transfers between devices: 13 us -> none  [shards(): lax.all_to_all(own_grad, 'fsdp', split_axis=1, concat_axis=0, tiled=True)]
  transfers between devices with their start and end apart: 6 -> 0, of which waited for: 3 -> 0; matrix products, arithmetic and copies ran while one was open for 5% -> 0% of each run, Pallas kernels for 0% -> 0%
where the time goes in v1:
time: 195 us; the launch traced here: 194 us
  Pallas kernels  135 us (69%)
  local copies, waits for them, and re-layouts  26.6 us (14%)
  matrix products  18.7 us (10%)
  other arithmetic  13.3 us (7%)
    pallas_call x1, Pallas kernels, gather_call(): pl.pallas_call(gather_kernel, out_shape=(jax.ShapeDtypeStruct((8, 128), F...  100 us
    pallas_call x1, Pallas kernels, reduce_call(): pl.pallas_call(reduce_kernel, out_shape=(jax.ShapeDtypeStruct((8, 128), F...  34.8 us
    slice x1, local copies, waits for them, and re-layouts, encode_backward(): value_all = jnp.dot(normed, weights[1], preferred_element_type=F32)  9.57 us
    unnamed x29, local copies, waits for them, and re-layouts  7.99 us
    dot_general x1, matrix products, encode_backward(): value_all = jnp.dot(normed, weights[1], preferred_element_type=F32)  7.05 us
    convert_element_type x2, other arithmetic, encode_backward(): normed = (wide * lax.rsqrt(jnp.mean(wide * wide, axis=-1, keepdims=True)...  5.49 us
    dot_general x5, matrix products, dot(): lax.dot_general(a, b, (((ca,), (cb,)), ((), ())), preferred_element_type=...  5.24 us

profile of v1, /device:TPU:1, one launch (start us, length us, event | category | flops | bytes accessed | tf_op | source)
XLA Modules:
  0.0 194.5 jit_solution(14546710022477445411)
XLA Ops:
  0.7 0.9 copy.29
  1.5 0.8 copy.30
  2.4 1.7 maximum_select_fusion.wh_in
  4.2 0.7 broadcast_in_dim.63
  5.1 0.7 reshape.261
  6.4 1.3 reshape.262.p_in
  7.8 100.1 %shard_map.180 = (f32[8,128]{1,0:T(8,128)}, f32[16,512]{1,0:T(8,128)}, f32[16,512]{1,0:T(8,128)}, f32[32,128]{1,0:T(8,128)}, bf16[2,16,2,4,2,16,640]{6,5,4,3,2,1,0:T(8,128)(2,1)}) custom-call(bf16[16,640]{1,0:T(8,128)(2,1)} %pad_maximum_fusion.2.q_in, bf16[16,512]{1,0:T(8,128)(2,1)} %reshape.262.p_in, bf16[128,128]{1,0:T(8,128)(2,1)} %wo_in.1, ...), custom_call_target="tpu_custom_call" | custom-call | tf_op jit(solution)/shard_map/pallas_call | solution.py:553
  107.9 9.6 %fusion.54 = (bf16[1,16,2,4,2,16,640]{6,5,4,3,2,1,0:T(8,128)(2,1)}, bf16[1,16,2,4,2,16,640]{6,5,4,3,2,1,0:T(8,128)(2,1)}) fusion(bf16[2,16,2,4,2,16,640]{6,5,4,3,2,1,0:T(8,128)(2,1)} %get-tuple-element.18), kind=kLoop, calls=%fused_computation.80 | loop fusion | bytes 20971520 | tf_op jit(solution)/shard_map/slice | solution.py:863
  117.4 3.2 %multiply_reduce_fusion = f32[2,256]{1,0:T(2,128)S(1)} fusion(bf16[2,256,4096]{2,1,0:T(8,128)(2,1)} %param.16), kind=kLoop, calls=%fused_computation.5 | loop fusion | flops 6290944 | bytes 4196352 | tf_op jit(solution)/shard_map/reduce_sum | solution.py:859
  120.9 1.7 multiply_convert_fusion
  122.6 0.8 copy-done.2
  123.4 3.4 %fusion.60 = f32[512,640]{1,0:T(8,128)S(1)} fusion(bf16[512,4096]{1,0:T(8,128)(2,1)S(1)} %bitcast.73, bf16[4096,640]{1,0:T(8,128)(2,1)S(1)} %bitcast.72), kind=kOutput, calls=%fused_computation.84 | convolution fusion | flops 2684354560 | bytes 10747904 | tf_op jit(solution)/shard_map/dot_general | solution.py:862
  126.8 1.1 copy-done.4
  130.5 7.1 %fusion.61 = f32[512,640]{1,0:T(8,128)S(1)} fusion(bf16[512,4096]{1,0:T(8,128)(2,1)} %bitcast.74, bf16[4096,640]{1,0:T(8,128)(2,1)} %bitcast.71), kind=kOutput, calls=%fused_computation.85 | convolution fusion | flops 2684354560 | bytes 10747904 | tf_op jit(solution)/shard_map/dot_general | solution.py:863
  137.6 1.1 copy-done.5
  139.7 0.9 fusion.4
  141.7 1.2 fusion.9
  143.9 1.2 fusion.10
  146.3 3.8 %fusion.2 = bf16[512,4096]{1,0:T(8,128)(2,1)S(1)} fusion(f32[4096]{0:T(1024)S(1)} %convert_element_type.66, f32[512]{0:T(512)S(1)} %bitcast.81, bf16[2,256,4096]{2,1,0:T(8,128)(2,1)} %param.16), kind=kLoop, calls=%fused_computation.3 | loop fusion | flops 8388608 | bytes 8407040 | tf_op jit(solution)/shard_map/convert_element_type | solution.py:861
  150.2 2.3 %fusion.3 = bf16[4096,128]{1,0:T(8,128)(2,1)} fusion(bf16[512,4096]{1,0:T(8,128)(2,1)S(1)} %fusion.2, bf16[512,64]{1,0:T(8,128)(2,1)S(1)} %convolution_convert_fusion.1, bf16[512,64]{1,0:T(8,128)(2,1)S(1)} %convolution_convert_fusion.2), kind=kOutput, calls=%fused_computation.7 | convolution fusion | flops 538181632 | bytes 5373952 | tf_op jit(solution)/shard_map/dot_general | solution.py:53
  152.5 34.8 %shard_map.181 = (f32[8,128]{1,0:T(8,128)}, f32[64,512]{1,0:T(8,128)}, f32[64,512]{1,0:T(8,128)}) custom-call(bf16[8,2,256,128]{3,2,1,0:T(8,128)(2,1)} %bitcast.70, bf16[2,16,16,128]{3,2,1,0:T(8,128)(2,1)} %bitcast.79), custom_call_target="tpu_custom_call" | custom-call | tf_op jit(solution)/shard_map/pallas_call | solution.py:812
  187.4 1.4 fusion.56
  191.4 1.6 copy.72
  192.9 1.6 copy.73
  (63 shorter events, 10.6 us)
Async XLA Ops:
  0.6 127.2 %copy-start = (bf16[64,512]{1,0:T(8,128)(2,1)S(1)}, bf16[64,512]{1,0:T(8,128)(2,1)}, u32[]{:S(2)}) copy-start(bf16[64,512]{1,0:T(8,128)(2,1)} %param.22) | copy-start | bytes 196612
  107.8 9.6 %copy-start.9 = (bf16[4096]{0:T(1024)(128)(2,1)S(1)}, bf16[4096]{0:T(1024)(128)(2,1)}, u32[]{:S(2)}) copy-start(bf16[4096]{0:T(1024)(128)(2,1)} %param.17) | copy-start | bytes 24580
  117.4 3.4 %copy-start.1 = (bf16[2,256,4096]{2,1,0:T(8,128)(2,1)S(1)}, bf16[2,256,4096]{2,1,0:T(8,128)(2,1)}, u32[]{:S(2)}) copy-start(bf16[2,256,4096]{2,1,0:T(8,128)(2,1)} %param.16) | copy-start | bytes 12582916
  120.9 2.5 %copy-start.2 = (bf16[1,16,2,4,2,16,640]{6,5,4,3,2,1,0:T(8,128)(2,1)S(1)}, bf16[1,16,2,4,2,16,640]{6,5,4,3,2,1,0:T(8,128)(2,1)}, u32[]{:S(2)}) copy-start(bf16[1,16,2,4,2,16,640]{6,5,4,3,2,1,0:T(8,128)(2,1)} %get-tuple-element.24) | copy-start | bytes 15728644
  122.6 4.2 %copy-start.3 = (bf16[2,256,4096]{2,1,0:T(8,128)(2,1)}, bf16[2,256,4096]{2,1,0:T(8,128)(2,1)S(1)}, u32[]{:S(2)}) copy-start(bf16[2,256,4096]{2,1,0:T(8,128)(2,1)S(1)} %multiply_convert_fusion) | copy-start | bytes 12582916
  126.8 1.1 copy-start.4
  128.5 1.4 copy-start.10
  130.5 8.1 %copy-start.11 = (bf16[64,512]{1,0:T(8,128)(2,1)S(1)}, bf16[64,512]{1,0:T(8,128)(2,1)}, u32[]{:S(2)}) copy-start(bf16[64,512]{1,0:T(8,128)(2,1)} %param.24) | copy-start | bytes 196612
  130.5 8.5 %copy-start.8 = (f32[32,128]{1,0:T(8,128)S(1)}, f32[32,128]{1,0:T(8,128)}, u32[]{:S(2)}) copy-start(f32[32,128]{1,0:T(8,128)} %get-tuple-element.19) | copy-start | bytes 49156
  137.6 1.1 copy-start.5
  150.2 39.9 %copy-start.7 = (f32[16,512]{1,0:T(8,128)S(1)}, f32[16,512]{1,0:T(8,128)}, u32[]{:S(2)}) copy-start(f32[16,512]{1,0:T(8,128)} %get-tuple-element.16) | copy-start | bytes 98308
  150.2 40.5 %copy-start.6 = (f32[16,512]{1,0:T(8,128)S(1)}, f32[16,512]{1,0:T(8,128)}, u32[]{:S(2)}) copy-start(f32[16,512]{1,0:T(8,128)} %get-tuple-element.17) | copy-start | bytes 98308

commit v2 on v0

v2 whole, which is shorter than its diff:
```python
import jax
import jax.numpy as jnp
import numpy as np
from jax import lax
from jax.experimental import pallas as pl
from jax.experimental.pallas import tpu as pltpu
from jax.sharding import PartitionSpec as P

F32 = jnp.float32
BF16 = jnp.bfloat16
MESH = pl.DeviceIdType.MESH
HEAD = 128
SCALE = 20.0
EPSILON = 1e-06
ROTARY_BASE = 1000000.0
VMEM_BYTES = 56 * 1024 * 1024
ROOT = HEAD ** (-0.5)


def position():
    b = lax.axis_index("batch")
    f = lax.axis_index("fsdp")
    y = b // 4
    xlo = (b // 2) % 2
    c = b % 2
    z = f // 2
    xhi = f % 2
    return (b, f, y, xlo, c, z, xhi)


def remote(src, dst, send_sem, recv_sem, b, f):
    return pltpu.make_async_remote_copy(
        src_ref=src,
        dst_ref=dst,
        send_sem=send_sem,
        recv_sem=recv_sem,
        device_id=(b, f),
        device_id_type=MESH,
    )


def loop(lo, hi, body):
    def step(i, carry):
        body(i)
        return carry

    lax.fori_loop(lo, hi, step, 0)


def iota(shape, dim):
    return lax.broadcasted_iota(jnp.int32, shape, dim)


def dot(a, b, ca=1, cb=0, precision=None):
    return lax.dot_general(
        a, b, (((ca,), (cb,)), ((), ())), preferred_element_type=F32, precision=precision
    )


def far_first(i):
    return 8 + (i // 2) * (2 * (i % 2) - 1)


INPUTS = (
    "q_in", "p_in", "pos_in", "hid_in", "gain_in", "lq_in", "fk_in", "fv_in",
    "kd_in", "ku_in", "vd_in", "vu_in", "wo_in", "cos_in", "sin_in",
)
OUTPUTS = ("loss_out", "qg_out", "pg_out", "dk_out", "dv_out", "uk_out", "uv_out")
BUFFERS = {
    "tmp": ((16, 512), F32),
    "lq": ((2, 16, 128), F32),
    "hid": ((512, 4096), BF16),
    "qs": ((2, 4, 4, 16, 640), BF16),
    "ps": ((16, 16, 512), BF16),
    "ws": ((2, 8, 16, 128), BF16),
    "wg": ((2, 2, 8, 128, 128), BF16),
    "qwg": ((16, 2, 32, 128), BF16),
    "st": ((32, 4, 128), F32),
    "pgs": ((16, 16, 512), BF16),
    "pgr": ((16, 16, 512), BF16),
    "hps": ((16, 32, 128), BF16),
    "hpr": ((16, 32, 128), BF16),
    "qgs": ((2, 16, 16, 512), BF16),
    "qgx": ((16, 16, 512), BF16),
    "qgr": ((16, 16, 512), BF16),
    "wk": ((4, 4, 2, 4, 2, 16, 640), BF16),
    "wv": ((4, 4, 2, 4, 2, 16, 512), BF16),
    "ku": ((128, 512), BF16),
    "vu": ((128, 512), BF16),
    "raw_k": ((512, 640), F32),
    "raw_v": ((512, 512), F32),
    "low": ((512, 128), BF16),
    "keys": ((512, 512), BF16),
    "values": ((512, 512), BF16),
    "back": ((128, 512), BF16),
    "att": ((2, 16, 256), F32),
    "dt": ((8, 2, 2, 128, 128), BF16),
    "d1": ((8, 2, 128, 128), BF16),
    "r1": ((16, 128, 128), BF16),
    "d2": ((16, 128, 128), BF16),
    "r2": ((16, 8, 128), F32),
    "d3": ((16, 8, 128), F32),
    "u0": ((2, 4, 64, 128), BF16),
    "u1": ((4, 64, 128), BF16),
    "v1": ((16, 16, 128), BF16),
    "u2": ((16, 16, 128), BF16),
    "v3": ((16, 128), F32),
    "u3": ((16, 16, 128), F32),
    "u4": ((16, 16, 128), F32),
    "u5": ((16, 16, 128), F32),
}
SEMAPHORES = {
    "hid_sem": (1,),
    "q1": (2, 4), "q2": (2, 4), "qx": (2, 4),
    "w1": (2, 4), "w2": (2, 4), "wx": (2, 8),
    "ax": (2, 4), "ay": (2, 4), "bx": (2, 4), "by": (2, 4),
    "p": (2, 16), "o1": (2, 16), "o2": (2, 16), "o3": (2,),
    "qw": (2, 16), "qwx": (2, 16), "sts": (2, 32),
    "pg": (2, 16), "hp": (2, 16), "qg": (2, 16), "qgc": (2,),
    "one": (2, 3), "sd2": (2, 16), "sd3": (2, 16),
    "su2": (2, 16), "su3": (2, 16), "su4": (2, 16),
}


class Refs:
    pass


def kernel(*refs):
    r = Refs()
    for name, ref in zip((*INPUTS, *OUTPUTS, *BUFFERS, *SEMAPHORES), refs, strict=True):
        setattr(r, name, ref)
    b, f, y, xlo, c, z, xhi = position()
    zh, zl = z // 4, z % 4
    pi = (b // 2) * 2 + xhi
    sib = b + 1 - 2 * c
    line = c * 16 + z
    OUT, IN = 0, 1

    def plane_dev(t):
        return ((t // 2) * 2 + c, z * 2 + t % 2)

    def line_dev(s):
        return ((b // 2) * 2 + s // 16, (s % 16) * 2 + xhi)

    def z_dev(zz):
        return (b, zz * 2 + xhi)

    def x_of(i):
        return (xhi * 2 + xlo + i) % 4

    def x_dev(i):
        x = x_of(i)
        return (y * 4 + (x % 2) * 2 + c, z * 2 + x // 2)

    def y_dev(i):
        return (((y + i) % 4) * 4 + xlo * 2 + c, f)

    def send(src, dst, sems, out, into, dev):
        return remote(src, dst, sems.at[OUT, out], sems.at[IN, into], dev[0], dev[1])

    def arrived(dst, sems, into):
        remote(dst, dst, sems.at[OUT, into], sems.at[IN, into], sib, f).wait_recv()

    hid_copy = pltpu.make_async_copy(r.hid_in, r.hid, r.hid_sem.at[0])
    hid_copy.start()
    barrier = pltpu.get_barrier_semaphore()

    def greet(dev):
        pl.semaphore_signal(barrier, inc=1, device_id=dev, device_id_type=MESH)

    def greet_line(i):
        zz = (z + far_first(i)) % 16
        greet(line_dev(zz))
        greet(line_dev(16 + zz))

    loop(1, 16, greet_line)
    loop(1, 16, lambda i: greet(plane_dev((pi + i) % 16)))
    greet((sib, f))

    def slab(ref):
        rows = ref[...].astype(F32)
        for j in range(2):
            for k in range(8):
                r.tmp[j * 8 + k : j * 8 + k + 1, :] = rows[j : j + 1, k * 512 : (k + 1) * 512]
        return r.tmp[...].astype(BF16)

    r.qs[c, zh, zl, :, 0:512] = slab(r.q_in)
    r.ps[pi] = slab(r.p_in)
    row, lane = iota((16, 128), 0), iota((16, 128), 1)
    mark = jnp.zeros((16, 128), F32)
    for j in range(2):
        spot = r.pos_in[j]
        high, low = (spot // 32).astype(F32), (spot % 32).astype(F32)
        mark = jnp.where((row == j * 8) & (lane == 0), high, mark)
        mark = jnp.where((row == j * 8) & (lane == 1), low, mark)
    r.qs[c, zh, zl, :, 512:640] = mark.astype(BF16)
    piece = pl.ds(pl.multiple_of((y * 2 + xlo) * 16, 16), 16)

    @pl.when(c == 0)
    def _():
        r.wk[zh, zl, xhi, y, xlo, :, 0:512] = r.fk_in[piece, :]
        r.wk[zh, zl, xhi, y, xlo, :, 512:640] = jnp.concatenate(
            [r.kd_in[piece, :], r.vd_in[piece, :]], axis=1
        )

    @pl.when(c == 1)
    def _():
        r.wv[zh, zl, xhi, y, xlo] = r.fv_in[piece, :]

    pl.semaphore_wait(barrier, 46)

    def far(i):
        return z_dev((z + 4 * i) % 16)

    def near(i):
        return z_dev((z + i - 4 * (i // 3)) % 16)

    def q1(i):
        own = r.qs.at[c, zh, zl]
        return send(own, own, r.q1, i, 4 - i, far(i))

    def q2(i):
        part = r.qs.at[c, :, zl]
        return send(part, part, r.q2, i, 4 - i, near(i))

    def qx(i):
        part = r.qs.at[c, :, (zl + i) % 4]
        return send(part, part, r.qx, i, i, (sib, f))

    loop(1, 4, lambda i: q1(i).start())

    mine = c == xlo

    def o1(zp):
        return send(
            r.wo_in.at[pl.ds(zp * 16, 16), :],
            r.ws.at[z % 2, z // 2],
            r.o1,
            zp,
            z,
            ((b // 2) * 2 + xlo, (2 * zp + c) * 2 + xhi),
        )

    def o1_start(zp):
        here = jnp.logical_and(mine, 2 * zp + c == z)

        @pl.when(jnp.logical_not(here))
        def _():
            o1(zp).start()

        @pl.when(here)
        def _():
            r.ws[z % 2, z // 2] = r.wo_in[pl.ds(zp * 16, 16), :]

    loop(0, 8, o1_start)

    def p_move(i):
        t = (pi + i) % 16
        return send(r.ps.at[pi], r.ps.at[pi], r.p, t, pi, plane_dev(t))

    def on_own(body):
        pl.when(c == 0)(lambda: body(r.wk))
        pl.when(c == 1)(lambda: body(r.wv))

    def on_other(body):
        pl.when(c == 0)(lambda: body(r.wv))
        pl.when(c == 1)(lambda: body(r.wk))

    def w1(w, i):
        own = w.at[zh, zl, xhi, y, xlo]
        return send(own, own, r.w1, i, 4 - i, far(i))

    def w2(w, i):
        part = w.at[:, zl, xhi, y, xlo]
        return send(part, part, r.w2, i, 4 - i, near(i))

    lo_z, hi_z = pl.ds(0, 2), pl.ds(2, 2)

    def ax(w, i):
        part = w.at[lo_z, :, xhi, y, xlo]
        return send(part, part, r.ax, i, 4 - i, x_dev(i))

    def by(w, i):
        part = w.at[hi_z, :, xhi, y, xlo]
        return send(part, part, r.by, i, 4 - i, y_dev(i))

    def ay(w, i):
        part = w.at[lo_z, :, :, y]
        return send(part, part, r.ay, i, 4 - i, y_dev(i))

    def bx(w, i):
        part = w.at[hi_z, :, xhi, :, xlo]
        return send(part, part, r.bx, i, 4 - i, x_dev(i))

    def wx_a(w, i):
        part = w.at[lo_z, :, :, (y + i) % 4]
        return send(part, part, r.wx, i, i, (sib, f))

    def wx_b(w, i):
        x = x_of(i)
        part = w.at[hi_z, :, x // 2, :, x % 2]
        return send(part, part, r.wx, 4 + i, 4 + i, (sib, f))

    on_own(lambda w: loop(1, 4, lambda i: w1(w, i).start()))
    loop(1, 16, lambda i: p_move(i).start())

    r.ku[0:64, :] = r.ku_in[...]
    r.ku[64:128, :] = jnp.zeros((64, 512), BF16)
    r.vu[0:64, :] = jnp.zeros((64, 512), BF16)
    r.vu[64:128, :] = r.vu_in[...]
    wide_q = r.lq_in[...].astype(F32)
    for j in range(2):
        for h in range(16):
            r.lq[j, h : h + 1, :] = wide_q[j : j + 1, h * 128 : (h + 1) * 128]

    hid_copy.wait()

    def norm(i):
        rows = pl.ds(pl.multiple_of(i * 32, 32), 32)
        x = r.hid[rows, :].astype(F32)
        scale = lax.rsqrt(jnp.mean(x * x, axis=1, keepdims=True) + EPSILON)
        r.hid[rows, :] = (x * scale * r.gain_in[...].astype(F32)).astype(BF16)

    loop(0, 8, norm)
    loop(1, 4, lambda i: arrived(r.qs.at[c, (zh + i) % 4, zl], r.q1, i))
    loop(1, 4, lambda i: q2(i).start())
    qx(0).start()

    def o2_slot(t, yy):
        return r.wg.at[:, t, :, pl.ds((c * 4 + yy) * 16, 16), :]

    def o2(i):
        t = (pi + i) % 16
        return send(r.ws, o2_slot(xhi, y), r.o2, t, y * 2 + xhi, plane_dev(t))

    @pl.when(mine)
    def _():
        def one(zz):
            @pl.when(jnp.logical_not(jnp.logical_and(z % 2 == c, zz == z)))
            def _():
                arrived(r.ws.at[zz % 2, zz // 2], r.o1, zz)

        loop(0, 16, one)
        loop(1, 16, lambda i: o2(i).start())
        r.wg[:, xhi, :, pl.ds((c * 4 + y) * 16, 16), :] = r.ws[...]

    def w1_done(w):
        loop(1, 4, lambda i: arrived(w.at[(zh + i) % 4, zl, xhi, y, xlo], r.w1, i))
        loop(1, 4, lambda i: w2(w, i).start())

    on_own(w1_done)
    loop(8, 16, norm)

    def q2_done(i):
        arrived(r.qs.at[c, :, (zl + i) % 4], r.q2, i)
        qx(i).start()

    loop(1, 4, q2_done)

    def w2_done(w):
        loop(1, 4, lambda i: arrived(w.at[:, (zl + i) % 4, xhi, y, xlo], r.w2, i))
        loop(1, 4, lambda i: ax(w, i).start())
        loop(1, 4, lambda i: by(w, i).start())

    on_own(w2_done)

    def p_done(i):
        t = (pi + i) % 16
        arrived(r.ps.at[t], r.p, t)

    loop(1, 16, p_done)
    loop(0, 4, lambda i: arrived(r.qs.at[1 - c, :, (zl + i) % 4], r.qx, i))
    q_all = r.qs[...].reshape(512, 640)
    q_rows = q_all[:, :512]
    p_rows = r.ps[...].reshape(256, 512)
    wide = dot(p_rows, q_rows, 1, 1).reshape(32, 8, 512)
    same = iota((32, 8, 512), 1) == iota((32, 8, 512), 2) % 8
    folded = jnp.sum(jnp.where(same, wide, 0.0), axis=1)
    fold = (iota((512, 64), 0) // 8 == iota((512, 64), 1)).astype(F32)
    scores = SCALE * dot(folded, fold, precision=lax.Precision.HIGHEST)
    marks = dot(q_all[:, 512:], fold.astype(BF16), 0, 0)
    target = marks[0:1] * 32.0 + marks[1:2]
    pid = iota((32, 64), 0)
    ptile = pid // 2
    ids = (((ptile // 2) * 2 + c) * 32 + z * 2 + ptile % 2) * 2 + pid % 2
    hit = (ids.astype(F32) == target).astype(F32)
    top = jnp.max(scores, axis=0, keepdims=True)
    local = top + jnp.log(jnp.sum(jnp.exp(scores - top), axis=0, keepdims=True))
    r.st[line] = jnp.zeros((4, 128), F32)
    r.st[line, 0:1, 0:64] = local
    r.st[line, 1:2, 0:64] = jnp.sum(scores * hit, axis=0, keepdims=True)

    def st_move(s):
        return send(r.st.at[line], r.st.at[line], r.sts, s, line, line_dev(s))

    def st_start(i):
        zz = (z + far_first(i)) % 16
        st_move(zz).start()
        st_move(16 + zz).start()

    loop(1, 16, st_start)
    st_move((1 - c) * 16 + z).start()

    half = r.wg.at[:, :, :, pl.ds(c * 64, 64), :]
    other = r.wg.at[:, :, :, pl.ds((1 - c) * 64, 64), :]

    def o2_done(s):
        @pl.when(jnp.logical_not(jnp.logical_and(mine, s == y * 2 + xhi)))
        def _():
            arrived(o2_slot(s % 2, s // 2), r.o2, s)

    loop(0, 8, o2_done)
    o3 = remote(half, half, r.o3.at[0], r.o3.at[1], sib, f)
    o3.start()
    remote(other, other, r.o3.at[0], r.o3.at[1], sib, f).wait_recv()
    q_half = r.qs[c].reshape(256, 640)
    prod = jnp.zeros((256, 1024), F32)
    for a in range(4):
        prod += dot(
            q_half[:, a * 128 : (a + 1) * 128], r.wg[a // 2, a % 2].reshape(1024, 128), 1, 1
        )
    qw = jnp.zeros((256, 128), F32)
    chunk = iota((256, 128), 0) % 8
    for a in range(8):
        qw += jnp.where(chunk == a, prod[:, a * 128 : (a + 1) * 128], 0.0)
    r.qwg[z, c] = jnp.sum(qw.reshape(32, 8, 128), axis=1).astype(BF16)

    def qw_move(i):
        zz = (z + far_first(i)) % 16
        return send(r.qwg.at[z, c], r.qwg.at[z, c], r.qw, zz, z, z_dev(zz))

    def qw_cross(zz):
        return send(r.qwg.at[zz, c], r.qwg.at[zz, c], r.qwx, zz, zz, (sib, f))

    loop(1, 16, lambda i: qw_move(i).start())
    qw_cross(z).start()

    def plane_done(w):
        def a_done(i):
            x = x_of(i)
            arrived(w.at[lo_z, :, x // 2, y, x % 2], r.ax, i)

        loop(1, 4, a_done)
        loop(1, 4, lambda i: ay(w, i).start())
        wx_a(w, 0).start()
        loop(1, 4, lambda i: arrived(w.at[hi_z, :, xhi, (y + i) % 4, xlo], r.by, i))
        loop(1, 4, lambda i: bx(w, i).start())
        wx_b(w, 0).start()

    on_own(plane_done)

    def st_done(i):
        s = (line + i) % 32
        arrived(r.st.at[s], r.sts, s)

    loop(1, 32, st_done)
    stats = r.st[...]
    peak = jnp.max(stats, axis=0)
    total = peak + jnp.log(jnp.sum(jnp.exp(stats - peak[None]), axis=0))
    picked = jnp.sum(stats, axis=0)
    lse = total[0:1, :64]
    weights = (jnp.exp(scores - lse) - hit).astype(BF16)

    def qw_done(i):
        zz = (z + far_first(16 - i)) % 16
        arrived(r.qwg.at[zz, c], r.qw, zz)
        qw_cross(zz).start()

    loop(1, 16, qw_done)
    loop(0, 16, lambda zz: arrived(r.qwg.at[zz, 1 - c], r.qwx, zz))
    rows16 = (iota((512, 32), 0) // 16 == iota((512, 32), 1)).astype(BF16)
    cols64 = (iota((64, 1024), 1) % 64 == iota((64, 1024), 0)).astype(BF16)
    tall = dot(dot(rows16, weights).astype(BF16), cols64)
    diag = iota((512, 1024), 0) % 16 == iota((512, 1024), 1) // 64
    tall = jnp.where(diag, tall, 0.0).astype(BF16)
    r.hps[...] = (
        (SCALE * dot(tall, r.qwg[...].reshape(1024, 128))).astype(BF16).reshape(16, 32, 128)
    )

    def hp_move(i):
        t = (pi + i) % 16
        return send(r.hps.at[t], r.hpr.at[pi], r.hp, t, pi, plane_dev(t))

    def pg_move(i):
        t = (pi + i) % 16
        return send(r.pgs.at[t], r.pgr.at[pi], r.pg, t, pi, plane_dev(t))

    loop(1, 16, lambda i: hp_move(i).start())
    r.hpr[pi] = r.hps[pi]
    rows8 = (iota((256, 32), 0) // 8 == iota((256, 32), 1)).astype(BF16)
    cols8 = (iota((64, 512), 1) // 8 == iota((64, 512), 0)).astype(BF16)
    spread = dot(dot(rows8, weights).astype(BF16), cols8)
    diag = iota((256, 512), 0) % 8 == iota((256, 512), 1) % 8
    spread = jnp.where(diag, spread, 0.0).astype(BF16)
    r.pgs[...] = (SCALE * dot(spread, q_rows)).astype(BF16).reshape(16, 16, 512)
    loop(1, 16, lambda i: pg_move(i).start())
    r.pgr[pi] = r.pgs[pi]

    r.qgs[...] = (SCALE * dot(spread, p_rows, 0, 0)).astype(BF16).reshape(2, 16, 16, 512)
    swap = remote(r.qgs.at[1 - c], r.qgx, r.qgc.at[0], r.qgc.at[1], sib, f)
    swap.start()
    loss = picked[1:2, :64]
    loss = lse - loss
    spot = iota((1, 64), 1)
    pick = [
        jnp.sum(jnp.where(spot == 2 * line + j, loss, 0.0), axis=1, keepdims=True)
        for j in range(2)
    ]
    r.loss_out[...] = jnp.where(iota((8, 128), 1) == 0, pick[0], pick[1])

    def qg_move(i):
        zz = (z + far_first(i)) % 16
        return send(r.qgs.at[c, zz], r.qgr.at[z], r.qg, zz, z, z_dev(zz))

    swap.wait_recv()
    r.qgs[c] = (r.qgs[c].astype(F32) + r.qgx[...].astype(F32)).astype(BF16)
    loop(1, 16, lambda i: qg_move(i).start())
    r.qgr[z] = r.qgs[c, z]

    def rows_done(w):
        def a_done(i):
            arrived(w.at[lo_z, :, :, (y + i) % 4], r.ay, i)
            wx_a(w, i).start()

        def b_done(i):
            x = x_of(i)
            arrived(w.at[hi_z, :, x // 2, :, x % 2], r.bx, i)
            wx_b(w, i).start()

        loop(1, 4, a_done)
        loop(1, 4, b_done)

    on_own(rows_done)

    def cross_done(w):
        def one(i):
            x = x_of(i)
            arrived(w.at[lo_z, :, :, (y + i) % 4], r.wx, i)
            arrived(w.at[hi_z, :, x // 2, :, x % 2], r.wx, 4 + i)

        loop(0, 4, one)

    on_other(cross_done)

    def project(w, raw, k):
        tokens = r.hid[:, pl.ds(pl.multiple_of(k * 1024, 1024), 1024)]
        part = dot(tokens, w[k].reshape(1024, w.shape[-1]))

        @pl.when(k == 0)
        def _():
            raw[...] = part

        @pl.when(k > 0)
        def _():
            raw[...] += part

    loop(0, 4, lambda k: project(r.wk, r.raw_k, k))
    r.low[...] = r.raw_k[:, 512:640].astype(BF16)
    adapted = dot(r.low[...], r.ku[...])
    own_group = iota((16, 512), 0) // 4 == iota((16, 512), 1) // 128

    def by_group(rows):
        return jnp.where(own_group, jnp.concatenate([rows] * 4, axis=1), 0.0).astype(BF16)

    queries = [by_group(r.lq[j]) for j in range(2)]
    for j in range(2):
        tok = slice(j * 256, (j + 1) * 256)
        for g in range(4):
            col = slice(g * 128, (g + 1) * 128)
            key = r.raw_k[tok, col] + 2.0 * adapted[tok, col]
            turned = pltpu.roll(key, 64, axis=1)
            r.keys[tok, col] = (key * r.cos_in[...] + turned * r.sin_in[...]).astype(BF16)
        sim = dot(queries[j], r.keys[tok, :], 1, 1) * ROOT
        sim = jnp.exp(sim - jnp.max(sim, axis=1, keepdims=True))
        r.att[j] = sim / jnp.sum(sim, axis=1, keepdims=True)

    loop(0, 4, lambda k: project(r.wv, r.raw_v, k))
    r.values[...] = (r.raw_v[...] + 2.0 * dot(r.low[...], r.vu[...])).astype(BF16)

    def hp_done(i):
        t = (pi + i) % 16
        arrived(r.hpr.at[t], r.hp, t)

    loop(1, 16, hp_done)
    heads = jnp.sum(r.hpr[...].astype(F32), axis=0).astype(BF16)
    row, lane = iota((128, 128), 0), iota((128, 128), 1)
    tile = (iota((128, 16), 0) % 16 == iota((128, 16), 1)).astype(BF16)
    group = (row % 16 == lane % 16).astype(BF16)
    head, src = iota((16, 128), 0), iota((16, 128), 1)
    place, at_z = src // 16, src % 16
    collect = (
        ((place % 4) * 4 + (place // 4) * 2 + at_z % 2 == head)
    ).astype(BF16)
    for j in range(2):
        tok = slice(j * 256, (j + 1) * 256)
        spread_rows = dot(tile, heads[j * 16 : (j + 1) * 16])
        spread_rows = jnp.where(lane // 16 == row // 16, spread_rows, 0.0).astype(BF16)
        copied = dot(spread_rows, group)
        copied = jnp.where(lane // 16 == (row % 16) // 2, copied, 0.0).astype(BF16)
        grads = by_group(dot(collect, copied))
        prob = dot(grads, r.values[tok, :], 1, 1)
        attention = r.att[j]
        expected = jnp.sum(attention * prob, axis=1, keepdims=True)
        score_grad = attention * (prob - expected)
        r.values[tok, :] = dot(attention.astype(BF16), grads, 0, 0).astype(BF16)
        turned_grad = dot(score_grad.astype(BF16), queries[j], 0, 0) * ROOT
        for g in range(4):
            col = slice(g * 128, (g + 1) * 128)
            part = turned_grad[:, col]
            turned = pltpu.roll(part, 64, axis=1)
            r.keys[tok, col] = (part * r.cos_in[...] - turned * r.sin_in[...]).astype(BF16)

    up_k = (2.0 * dot(r.low[...], r.keys[...], 0, 0)).astype(BF16)
    up_v = (2.0 * dot(r.low[...], r.values[...], 0, 0)).astype(BF16)
    for k in range(4):
        r.u0[0, k] = up_k[0:64, k * 128 : (k + 1) * 128]
        r.u0[1, k] = up_v[64:128, k * 128 : (k + 1) * 128]
    u_swap = send(r.u0.at[1 - c], r.u1, r.one, 0, 0, (sib, f))
    u_swap.start()
    back = dot(r.keys[...], r.ku[...], 1, 1) + dot(r.values[...], r.vu[...], 1, 1)
    r.back[...] = jnp.transpose(back.astype(BF16).astype(F32)).astype(BF16)

    def down(j, cc):
        cols = pl.ds(pl.multiple_of((j * 2 + cc) * 256, 256), 256)
        part = (2.0 * dot(r.back[...], r.hid[:, cols])).astype(BF16)
        r.dt[j, cc, 0] = part[:, :128]
        r.dt[j, cc, 1] = part[:, 128:]

    loop(0, 8, lambda j: down(j, 1 - c))
    d_swap = send(r.dt.at[:, 1 - c], r.d1, r.one, 1, 1, (sib, f))
    d_swap.start()
    u_swap.wait_recv()
    r.v1[...] = (
        (r.u0[c].astype(F32) + r.u1[...].astype(F32)).astype(BF16).reshape(16, 16, 128)
    )

    def u2_move(i):
        t = (pi + i) % 16
        return send(r.v1.at[t], r.u2.at[pi], r.su2, t, pi, plane_dev(t))

    def d2_move(i):
        t = (pi + i) % 16
        return send(r.r1.at[t], r.d2.at[pi], r.sd2, t, pi, plane_dev(t))

    loop(1, 16, lambda i: u2_move(i).start())
    r.u2[pi] = r.v1[pi]
    loop(0, 8, lambda j: down(j, c))
    d_swap.wait_recv()
    r.r1[...] = (
        (r.dt[:, c].astype(F32) + r.d1[...].astype(F32)).astype(BF16).reshape(16, 128, 128)
    )
    loop(1, 16, lambda i: d2_move(i).start())
    r.d2[pi] = r.r1[pi]

    def u2_done(i):
        t = (pi + i) % 16
        arrived(r.u2.at[t], r.su2, t)

    loop(1, 16, u2_done)
    r.v3[...] = jnp.sum(r.u2[...].astype(F32), axis=0)
    r.u3[z] = r.v3[...]

    def u3_move(i):
        zz = (z + far_first(i)) % 16
        return send(r.v3, r.u3.at[z], r.su3, zz, z, z_dev(zz))

    loop(1, 16, lambda i: u3_move(i).start())

    def d2_done(i):
        t = (pi + i) % 16
        arrived(r.d2.at[t], r.sd2, t)

    loop(1, 16, d2_done)
    r.r2[...] = jnp.transpose(jnp.sum(r.d2[...].astype(F32), axis=0)).reshape(16, 8, 128)

    def d3_move(k):
        return send(
            r.r2.at[k], r.d3.at[z], r.sd3, k, z, (b, (8 * xhi + k // 2) * 2 + k % 2)
        )

    def d3_self(k):
        return (8 * xhi + k // 2) * 2 + k % 2 == f

    def d3_start(k):
        @pl.when(jnp.logical_not(d3_self(k)))
        def _():
            d3_move(k).start()

        @pl.when(d3_self(k))
        def _():
            r.d3[z] = r.r2[k]

    loop(0, 16, d3_start)

    def put_rows(out, total):
        r.tmp[...] = total
        for j in range(2):
            for k in range(8):
                out[j : j + 1, k * 512 : (k + 1) * 512] = r.tmp[j * 8 + k : j * 8 + k + 1, :]

    def pg_done(i):
        t = (pi + i) % 16
        arrived(r.pgr.at[t], r.pg, t)

    def qg_done(i):
        t = (z + i) % 16
        arrived(r.qgr.at[t], r.qg, t)

    loop(1, 16, pg_done)
    put_rows(r.pg_out, jnp.sum(r.pgr[...].astype(F32), axis=0))
    loop(1, 16, qg_done)
    put_rows(r.qg_out, jnp.sum(r.qgr[...].astype(F32), axis=0))

    def u3_done(i):
        t = (z + i) % 16
        arrived(r.u3.at[t], r.su3, t)

    loop(1, 16, u3_done)
    r.u4[pi] = jnp.sum(r.u3[...], axis=0)

    def u4_move(i):
        t = (pi + i) % 16
        return send(r.u4.at[pi], r.u4.at[pi], r.su4, t, pi, plane_dev(t))

    loop(1, 16, lambda i: u4_move(i).start())

    def d3_done(zz):
        @pl.when(jnp.logical_not(jnp.logical_and(z // 8 == xhi, zz == z)))
        def _():
            arrived(r.d3.at[zz], r.sd3, zz)

    loop(0, 16, d3_done)
    down_total = jnp.sum(r.d3[...], axis=0)
    r.dk_out[...] = down_total[:, :64]
    r.dv_out[...] = down_total[:, 64:]

    def u4_done(i):
        t = (pi + i) % 16
        arrived(r.u4.at[t], r.su4, t)

    loop(1, 16, u4_done)
    u_back = send(r.u4, r.u5, r.one, 2, 2, (sib, f))
    u_back.start()

    def z_sent(i):
        q1(i).wait_send()
        q2(i).wait_send()

    loop(1, 4, z_sent)
    loop(0, 4, lambda i: qx(i).wait_send())

    def rows_sent(w):
        def one(i):
            w1(w, i).wait_send()
            w2(w, i).wait_send()
            ax(w, i).wait_send()
            ay(w, i).wait_send()
            bx(w, i).wait_send()
            by(w, i).wait_send()

        def two(i):
            wx_a(w, i).wait_send()
            wx_b(w, i).wait_send()

        loop(1, 4, one)
        loop(0, 4, two)

    on_own(rows_sent)

    def o1_sent(zp):
        @pl.when(jnp.logical_not(jnp.logical_and(mine, 2 * zp + c == z)))
        def _():
            o1(zp).wait_send()

    loop(0, 8, o1_sent)

    @pl.when(mine)
    def _():
        loop(1, 16, lambda i: o2(i).wait_send())

    o3.wait_send()
    swap.wait_send()
    u_swap.wait_send()
    d_swap.wait_send()

    def sixteen_sent(i):
        p_move(i).wait_send()
        qw_move(i).wait_send()
        pg_move(i).wait_send()
        hp_move(i).wait_send()
        qg_move(i).wait_send()
        u2_move(i).wait_send()
        d2_move(i).wait_send()
        u3_move(i).wait_send()
        u4_move(i).wait_send()

    loop(1, 16, sixteen_sent)

    def more_sent(k):
        qw_cross(k).wait_send()

        @pl.when(jnp.logical_not(d3_self(k)))
        def _():
            d3_move(k).wait_send()

    loop(0, 16, more_sent)
    loop(1, 32, lambda i: st_move((line + i) % 32).wait_send())

    u_back.wait_recv()

    def put(out, src):
        full = src[...].reshape(256, 128)
        for k in range(4):
            out[:, k * 128 : (k + 1) * 128] = full[k * 64 : (k + 1) * 64]

    @pl.when(c == 0)
    def _():
        put(r.uk_out, r.u4)
        put(r.uv_out, r.u5)

    @pl.when(c == 1)
    def _():
        put(r.uk_out, r.u5)
        put(r.uv_out, r.u4)

    u_back.wait_send()


def rotary_tables(length):
    half = HEAD // 2
    frequency = ROTARY_BASE ** (-(np.arange(half) * 2.0 / HEAD))
    angles = np.arange(length)[:, None] * frequency[None, :]
    cosine, sine = np.cos(angles), np.sin(angles)
    return (
        np.concatenate([cosine, cosine], axis=1).astype(np.float32),
        np.concatenate([-sine, sine], axis=1).astype(np.float32),
    )


def shards(
    queries,
    passages,
    positives,
    hidden,
    norm_gain,
    last_query,
    frozen_key_weight,
    frozen_value_weight,
    key_down,
    key_adapter_up,
    value_down,
    value_adapter_up,
    out_weight,
):
    vm = pl.BlockSpec(memory_space=pltpu.VMEM)
    specs = [vm] * len(INPUTS)
    specs[INPUTS.index("pos_in")] = pl.BlockSpec(memory_space=pltpu.SMEM)
    specs[INPUTS.index("hid_in")] = pl.BlockSpec(memory_space=pl.ANY)
    shapes = ((8, 128), (2, 4096), (2, 4096), (8, 64), (8, 64), (64, 512), (64, 512))
    cosine, sine = rotary_tables(256)
    loss, q_grad, p_grad, down_key, down_value, up_key, up_value = pl.pallas_call(
        kernel,
        out_shape=tuple(jax.ShapeDtypeStruct(shape, F32) for shape in shapes),
        in_specs=specs,
        out_specs=(vm,) * len(shapes),
        scratch_shapes=[pltpu.VMEM(shape, dtype) for shape, dtype in BUFFERS.values()]
        + [pltpu.SemaphoreType.DMA(shape) for shape in SEMAPHORES.values()],
        compiler_params=pltpu.CompilerParams(
            collective_id=0, has_side_effects=True, vmem_limit_bytes=VMEM_BYTES
        ),
    )(
        queries,
        passages,
        positives,
        hidden.reshape(512, 4096),
        norm_gain.reshape(1, 4096),
        last_query,
        frozen_key_weight,
        frozen_value_weight,
        key_down,
        key_adapter_up,
        value_down,
        value_adapter_up,
        out_weight,
        cosine,
        sine,
    )
    return (loss[0, :2], q_grad, p_grad, down_key, down_value, up_key, up_value)


def solution(mesh):
    rows = P(("batch", "fsdp"), None)
    placed = (
        rows,
        rows,
        P(("batch", "fsdp")),
        P(("batch", "fsdp"), None, None),
        P(),
        rows,
        P("fsdp", None),
        P("fsdp", None),
        P("fsdp", None),
        P(),
        P("fsdp", None),
        P(),
        P("batch", "fsdp"),
    )
    return jax.shard_map(
        shards,
        mesh=mesh,
        in_specs=placed,
        out_specs=(P(("batch", "fsdp")), rows, rows, rows, rows, P(), P()),
        check_vma=False,
    )
```

time: 1290 us -> 139 us (0.11)
  waiting for transfers between devices: 615 us -> 0 us
  blocking collectives: 577 us -> 0 us
  Pallas kernels: 0 us -> 124 us
  matrix products: 44.2 us -> 0 us
  between operations: 17.8 us -> 0.64 us
    unnamed x8 -> x0, waiting for transfers between devices: 602 us -> none
    all_gather x5 -> x0, blocking collectives: 312 us -> none  [the longest x1 80.7 us: shards(): output_block = lax.all_gather(out_weight, 'batch', axis=0, tiled=True)]
    psum x2 -> x0, blocking collectives: 189 us -> none  [shards(): lax.psum((jnp.sum(exponent, axis=1), jnp.sum(similarity_scores * onehot,...]
    pallas_call x0 -> x1, Pallas kernels: none -> 124 us  [shards(): pl.pallas_call(kernel, out_shape=tuple((jax.ShapeDtypeStruct(shape, F32)...]
    pmax x1 -> x0, blocking collectives: 58.1 us -> none  [shards(): row_max = lax.pmax(jnp.max(similarity_scores, axis=1), 'fsdp')]
    dot_general x32 -> x0, matrix products: 44.2 us -> none  [the longest x2 7.54 us: encode_backward(): jnp.dot(normed, frozen_key_weight, preferred_element_type=jnp.float32)]
    unnamed x1 -> x0, blocking collectives: 18.2 us -> none
    all_to_all x1 -> x0, waiting for transfers between devices: 13 us -> none  [shards(): lax.all_to_all(own_grad, 'fsdp', split_axis=1, concat_axis=0, tiled=True)]
  transfers between devices with their start and end apart: 6 -> 0, of which waited for: 3 -> 0; matrix products, arithmetic and copies ran while one was open for 5% -> 0% of each run, Pallas kernels for 0% -> 0%
where the time goes in v2:
time: 139 us; the launch traced here: 138 us
  Pallas kernels  124 us (89%)
  local copies, waits for them, and re-layouts  13.8 us (10%)
    pallas_call x1, Pallas kernels, shards(): pl.pallas_call(kernel, out_shape=tuple((jax.ShapeDtypeStruct(shape, F32)...  124 us
    unnamed x8, local copies, waits for them, and re-layouts  11.3 us

profile of v2, /device:TPU:1, one launch (start us, length us, event | category | flops | bytes accessed | tf_op | source)
XLA Modules:
  0.0 138.0 jit_solution(4619392224538877467)
XLA Ops:
  0.6 1.3 reshape.21.refs_4_
  1.9 1.4 %copy.22.refs_8_ = bf16[128,64]{1,0:T(8,128)(2,1)} copy(bf16[128,64]{0,1:T(8,128)(2,1)} %param.23) | data formatting | bytes 32768 | tf_op args[8]
  3.4 1.4 %copy.23.refs_10_ = bf16[128,64]{1,0:T(8,128)(2,1)} copy(bf16[128,64]{0,1:T(8,128)(2,1)} %param.25) | data formatting | bytes 32768 | tf_op args[10]
  4.8 123.6 %shard_map.198 = (f32[8,128]{1,0:T(8,128)}, f32[2,4096]{1,0:T(2,128)}, f32[2,4096]{1,0:T(2,128)}, f32[8,64]{1,0:T(8,128)}, f32[8,64]{1,0:T(8,128)}, /*index=5*/f32[64,512]{1,0:T(8,128)}, f32[64,512]{1,0:T(8,128)}) custom-call(bf16[2,4096]{1,0:T(2,128)(2,1)} %refs_0_.1, bf16[2,4096]{1,0:T(2,128)(2,1)} %refs_1_.1, s32[2]{0:T(128)} %refs_2_.1, ...), custom_call_target="tpu_custom_call" | custom-call | tf_op jit(solution)/shard_map/pallas_call | solution.py:862
  128.4 1.2 slice_bitcast_fusion
  129.6 1.4 copy.30
  130.9 1.4 copy.31
  132.3 1.3 copy.32
  133.6 1.3 copy.33
  134.9 1.6 %copy.34 = f32[64,512]{1,0:T(8,128)} copy(f32[64,512]{1,0:T(8,128)} %get-tuple-element.33) | data formatting | bytes 262144
  136.4 1.6 %copy.35 = f32[64,512]{1,0:T(8,128)} copy(f32[64,512]{1,0:T(8,128)} %get-tuple-element.34) | data formatting | bytes 262144

commit v3 on v2

--- a/solution.py
+++ b/solution.py
@@ -85,6 +85,7 @@
     "qgr": ((16, 16, 512), BF16),
     "wk": ((4, 4, 2, 4, 2, 16, 640), BF16),
     "wv": ((4, 4, 2, 4, 2, 16, 512), BF16),
+    "dn": ((128, 128), BF16),
     "ku": ((128, 512), BF16),
     "vu": ((128, 512), BF16),
     "raw_k": ((512, 640), F32),
@@ -92,6 +93,8 @@
     "low": ((512, 128), BF16),
     "keys": ((512, 512), BF16),
     "values": ((512, 512), BF16),
+    "vg": ((512, 512), BF16),
+    "gq": ((2, 16, 512), BF16),
     "back": ((128, 512), BF16),
     "att": ((2, 16, 256), F32),
     "dt": ((8, 2, 2, 128, 128), BF16),
@@ -113,7 +116,7 @@
     "hid_sem": (1,),
     "q1": (2, 4), "q2": (2, 4), "qx": (2, 4),
     "w1": (2, 4), "w2": (2, 4), "wx": (2, 8),
-    "ax": (2, 4), "ay": (2, 4), "bx": (2, 4), "by": (2, 4),
+    "ax": (2, 4), "ay": (2, 6), "bx": (2, 6), "by": (2, 4),
     "p": (2, 16), "o1": (2, 16), "o2": (2, 16), "o3": (2,),
     "qw": (2, 16), "qwx": (2, 16), "sts": (2, 32),
     "pg": (2, 16), "hp": (2, 16), "qg": (2, 16), "qgc": (2,),
@@ -200,9 +203,9 @@
     @pl.when(c == 0)
     def _():
         r.wk[zh, zl, xhi, y, xlo, :, 0:512] = r.fk_in[piece, :]
-        r.wk[zh, zl, xhi, y, xlo, :, 512:640] = jnp.concatenate(
-            [r.kd_in[piece, :], r.vd_in[piece, :]], axis=1
-        )
+        downs = jnp.concatenate([r.kd_in[...], r.vd_in[...]], axis=0).astype(F32)
+        r.dn[...] = jnp.transpose(downs).astype(BF16)
+        r.wk[zh, zl, xhi, y, xlo, :, 512:640] = r.dn[piece, :]
 
     @pl.when(c == 1)
     def _():
@@ -227,8 +230,6 @@
     def qx(i):
         part = r.qs.at[c, :, (zl + i) % 4]
         return send(part, part, r.qx, i, i, (sib, f))
-
-    loop(1, 4, lambda i: q1(i).start())
 
     mine = c == xlo
 
@@ -254,6 +255,7 @@
             r.ws[z % 2, z // 2] = r.wo_in[pl.ds(zp * 16, 16), :]
 
     loop(0, 8, o1_start)
+    loop(1, 4, lambda i: q1(i).start())
 
     def p_move(i):
         t = (pi + i) % 16
@@ -271,6 +273,9 @@
         own = w.at[zh, zl, xhi, y, xlo]
         return send(own, own, r.w1, i, 4 - i, far(i))
 
+    def w1_start(w):
+        loop(1, 4, lambda i: w1(w, i).start())
+
     def w2(w, i):
         part = w.at[:, zl, xhi, y, xlo]
         return send(part, part, r.w2, i, 4 - i, near(i))
@@ -285,13 +290,22 @@
         part = w.at[hi_z, :, xhi, y, xlo]
         return send(part, part, r.by, i, 4 - i, y_dev(i))
 
-    def ay(w, i):
-        part = w.at[lo_z, :, :, y]
-        return send(part, part, r.ay, i, 4 - i, y_dev(i))
-
-    def bx(w, i):
-        part = w.at[hi_z, :, xhi, :, xlo]
-        return send(part, part, r.bx, i, 4 - i, x_dev(i))
+    def a_part(w, i, h):
+        return w.at[h, :, :, (y + i) % 4]
+
+    def b_part(w, i, h):
+        x = x_of(i)
+        return w.at[2 + h, :, x // 2, :, x % 2]
+
+    def own_on(w, part, sems, dev, d, h):
+        own = part(w, 0, h)
+        return send(own, own, sems, d * 2 + h, d * 2 + h, dev(1 + 2 * d))
+
+    def pass_on(w, part, sems, dev, d):
+        got = part(w, 3 - 2 * d, 1 - d)
+        return send(got, got, sems, 4 + d, 4 + d, dev(1 + 2 * d))
+
+    rings = ((a_part, r.ay, y_dev), (b_part, r.bx, x_dev))
 
     def wx_a(w, i):
         part = w.at[lo_z, :, :, (y + i) % 4]
@@ -302,7 +316,7 @@
         part = w.at[hi_z, :, x // 2, :, x % 2]
         return send(part, part, r.wx, 4 + i, 4 + i, (sib, f))
 
-    on_own(lambda w: loop(1, 4, lambda i: w1(w, i).start()))
+    pl.when(c == 0)(lambda: w1_start(r.wk))
     loop(1, 16, lambda i: p_move(i).start())
 
     r.ku[0:64, :] = r.ku_in[...]
@@ -349,7 +363,8 @@
         loop(1, 4, lambda i: arrived(w.at[(zh + i) % 4, zl, xhi, y, xlo], r.w1, i))
         loop(1, 4, lambda i: w2(w, i).start())
 
-    on_own(w1_done)
+    pl.when(c == 0)(lambda: w1_done(r.wk))
+    pl.when(c == 1)(lambda: w1_start(r.wv))
     loop(8, 16, norm)
 
     def q2_done(i):
@@ -360,10 +375,66 @@
 
     def w2_done(w):
         loop(1, 4, lambda i: arrived(w.at[:, (zl + i) % 4, xhi, y, xlo], r.w2, i))
+
+    def first_start(w):
         loop(1, 4, lambda i: ax(w, i).start())
         loop(1, 4, lambda i: by(w, i).start())
 
-    on_own(w2_done)
+    def first_done(w):
+        def a_done(i):
+            x = x_of(i)
+            arrived(w.at[lo_z, :, x // 2, y, x % 2], r.ax, i)
+
+        loop(1, 4, a_done)
+        loop(1, 4, lambda i: arrived(w.at[hi_z, :, xhi, (y + i) % 4, xlo], r.by, i))
+
+    def second_start(w):
+        for part, sems, dev in rings:
+            own_on(w, part, sems, dev, 0, 1).start()
+            own_on(w, part, sems, dev, 1, 0).start()
+        for part, sems, dev in rings:
+            own_on(w, part, sems, dev, 0, 0).start()
+            own_on(w, part, sems, dev, 1, 1).start()
+        wx_a(w, 0).start()
+        wx_b(w, 0).start()
+
+    def second_pass(w):
+        for part, sems, dev in rings:
+            arrived(part(w, 3, 1), sems, 1)
+            pass_on(w, part, sems, dev, 0).start()
+            arrived(part(w, 1, 0), sems, 2)
+            pass_on(w, part, sems, dev, 1).start()
+
+    def second_done(w):
+        for (part, sems, dev), cross in zip(rings, (wx_a, wx_b)):
+            arrived(part(w, 3, 0), sems, 0)
+            cross(w, 3).start()
+            arrived(part(w, 1, 1), sems, 3)
+            cross(w, 1).start()
+        for (part, sems, dev), cross in zip(rings, (wx_a, wx_b)):
+            arrived(part(w, 2, 1), sems, 4)
+            arrived(part(w, 2, 0), sems, 5)
+            cross(w, 2).start()
+
+    def cross_a_done(w):
+        loop(0, 4, lambda i: arrived(w.at[lo_z, :, :, (y + i) % 4], r.wx, i))
+
+    def cross_b_done(w):
+        def one(i):
+            x = x_of(i)
+            arrived(w.at[hi_z, :, x // 2, :, x % 2], r.wx, 4 + i)
+
+        loop(0, 4, one)
+
+    def keys_core(body):
+        pl.when(c == 0)(lambda: body(r.wk))
+
+    def values_core(body):
+        pl.when(c == 1)(lambda: body(r.wv))
+
+    keys_core(w2_done)
+    keys_core(first_start)
+    values_core(w1_done)
 
     def p_done(i):
         t = (pi + i) % 16
@@ -413,6 +484,10 @@
     loop(0, 8, o2_done)
     o3 = remote(half, half, r.o3.at[0], r.o3.at[1], sib, f)
     o3.start()
+    keys_core(first_done)
+    keys_core(second_start)
+    values_core(w2_done)
+    values_core(first_start)
     remote(other, other, r.o3.at[0], r.o3.at[1], sib, f).wait_recv()
     q_half = r.qs[c].reshape(256, 640)
     prod = jnp.zeros((256, 1024), F32)
@@ -436,20 +511,7 @@
     loop(1, 16, lambda i: qw_move(i).start())
     qw_cross(z).start()
 
-    def plane_done(w):
-        def a_done(i):
-            x = x_of(i)
-            arrived(w.at[lo_z, :, x // 2, y, x % 2], r.ax, i)
-
-        loop(1, 4, a_done)
-        loop(1, 4, lambda i: ay(w, i).start())
-        wx_a(w, 0).start()
-        loop(1, 4, lambda i: arrived(w.at[hi_z, :, xhi, (y + i) % 4, xlo], r.by, i))
-        loop(1, 4, lambda i: bx(w, i).start())
-        wx_b(w, 0).start()
-
-    on_own(plane_done)
-
+    keys_core(second_pass)
     def st_done(i):
         s = (line + i) % 32
         arrived(r.st.at[s], r.sts, s)
@@ -488,6 +550,8 @@
 
     loop(1, 16, lambda i: hp_move(i).start())
     r.hpr[pi] = r.hps[pi]
+    values_core(first_done)
+    values_core(second_start)
     rows8 = (iota((256, 32), 0) // 8 == iota((256, 32), 1)).astype(BF16)
     cols8 = (iota((64, 512), 1) // 8 == iota((64, 512), 0)).astype(BF16)
     spread = dot(dot(rows8, weights).astype(BF16), cols8)
@@ -503,46 +567,22 @@
     loss = picked[1:2, :64]
     loss = lse - loss
     spot = iota((1, 64), 1)
-    pick = [
-        jnp.sum(jnp.where(spot == 2 * line + j, loss, 0.0), axis=1, keepdims=True)
-        for j in range(2)
-    ]
-    r.loss_out[...] = jnp.where(iota((8, 128), 1) == 0, pick[0], pick[1])
+    for j in range(2):
+        r.loss_out[j] = jnp.sum(jnp.where(spot == 2 * line + j, loss, 0.0))
 
     def qg_move(i):
         zz = (z + far_first(i)) % 16
         return send(r.qgs.at[c, zz], r.qgr.at[z], r.qg, zz, z, z_dev(zz))
 
+    keys_core(second_done)
+    values_core(second_pass)
     swap.wait_recv()
     r.qgs[c] = (r.qgs[c].astype(F32) + r.qgx[...].astype(F32)).astype(BF16)
     loop(1, 16, lambda i: qg_move(i).start())
     r.qgr[z] = r.qgs[c, z]
 
-    def rows_done(w):
-        def a_done(i):
-            arrived(w.at[lo_z, :, :, (y + i) % 4], r.ay, i)
-            wx_a(w, i).start()
-
-        def b_done(i):
-            x = x_of(i)
-            arrived(w.at[hi_z, :, x // 2, :, x % 2], r.bx, i)
-            wx_b(w, i).start()
-
-        loop(1, 4, a_done)
-        loop(1, 4, b_done)
-
-    on_own(rows_done)
-
-    def cross_done(w):
-        def one(i):
-            x = x_of(i)
-            arrived(w.at[lo_z, :, :, (y + i) % 4], r.wx, i)
-            arrived(w.at[hi_z, :, x // 2, :, x % 2], r.wx, 4 + i)
-
-        loop(0, 4, one)
-
-    on_other(cross_done)
-
+    pl.when(c == 1)(lambda: cross_a_done(r.wk))
+    pl.when(c == 1)(lambda: cross_b_done(r.wk))
     def project(w, raw, k):
         tokens = r.hid[:, pl.ds(pl.multiple_of(k * 1024, 1024), 1024)]
         part = dot(tokens, w[k].reshape(1024, w.shape[-1]))
@@ -575,9 +615,7 @@
         sim = jnp.exp(sim - jnp.max(sim, axis=1, keepdims=True))
         r.att[j] = sim / jnp.sum(sim, axis=1, keepdims=True)
 
-    loop(0, 4, lambda k: project(r.wv, r.raw_v, k))
-    r.values[...] = (r.raw_v[...] + 2.0 * dot(r.low[...], r.vu[...])).astype(BF16)
-
+    values_core(second_done)
     def hp_done(i):
         t = (pi + i) % 16
         arrived(r.hpr.at[t], r.hp, t)
@@ -598,12 +636,28 @@
         spread_rows = jnp.where(lane // 16 == row // 16, spread_rows, 0.0).astype(BF16)
         copied = dot(spread_rows, group)
         copied = jnp.where(lane // 16 == (row % 16) // 2, copied, 0.0).astype(BF16)
-        grads = by_group(dot(collect, copied))
-        prob = dot(grads, r.values[tok, :], 1, 1)
+        r.gq[j] = by_group(dot(collect, copied))
+        r.vg[tok, :] = dot(r.att[j].astype(BF16), r.gq[j], 0, 0).astype(BF16)
+    up_v = (2.0 * dot(r.low[...], r.vg[...], 0, 0)).astype(BF16)
+    for k in range(4):
+        r.u0[1, k] = up_v[64:128, k * 128 : (k + 1) * 128]
+    r.raw_v[...] = 2.0 * dot(r.low[...], r.vu[...])
+
+    def project_values(k):
+        tokens = r.hid[:, pl.ds(pl.multiple_of(k * 1024, 1024), 1024)]
+        r.raw_v[...] += dot(tokens, r.wv[k].reshape(1024, 512))
+
+    pl.when(c == 0)(lambda: cross_a_done(r.wv))
+    loop(0, 2, project_values)
+    pl.when(c == 0)(lambda: cross_b_done(r.wv))
+    loop(2, 4, project_values)
+    r.values[...] = r.raw_v[...].astype(BF16)
+    for j in range(2):
+        tok = slice(j * 256, (j + 1) * 256)
+        prob = dot(r.gq[j], r.values[tok, :], 1, 1)
         attention = r.att[j]
         expected = jnp.sum(attention * prob, axis=1, keepdims=True)
         score_grad = attention * (prob - expected)
-        r.values[tok, :] = dot(attention.astype(BF16), grads, 0, 0).astype(BF16)
         turned_grad = dot(score_grad.astype(BF16), queries[j], 0, 0) * ROOT
         for g in range(4):
             col = slice(g * 128, (g + 1) * 128)
@@ -612,13 +666,11 @@
             r.keys[tok, col] = (part * r.cos_in[...] - turned * r.sin_in[...]).astype(BF16)
 
     up_k = (2.0 * dot(r.low[...], r.keys[...], 0, 0)).astype(BF16)
-    up_v = (2.0 * dot(r.low[...], r.values[...], 0, 0)).astype(BF16)
     for k in range(4):
         r.u0[0, k] = up_k[0:64, k * 128 : (k + 1) * 128]
-        r.u0[1, k] = up_v[64:128, k * 128 : (k + 1) * 128]
     u_swap = send(r.u0.at[1 - c], r.u1, r.one, 0, 0, (sib, f))
     u_swap.start()
-    back = dot(r.keys[...], r.ku[...], 1, 1) + dot(r.values[...], r.vu[...], 1, 1)
+    back = dot(r.keys[...], r.ku[...], 1, 1) + dot(r.vg[...], r.vu[...], 1, 1)
     r.back[...] = jnp.transpose(back.astype(BF16).astype(F32)).astype(BF16)
 
     def down(j, cc):
@@ -755,8 +807,6 @@
             w1(w, i).wait_send()
             w2(w, i).wait_send()
             ax(w, i).wait_send()
-            ay(w, i).wait_send()
-            bx(w, i).wait_send()
             by(w, i).wait_send()
 
         def two(i):
@@ -765,6 +815,11 @@
 
         loop(1, 4, one)
         loop(0, 4, two)
+        for part, sems, dev in rings:
+            for d in range(2):
+                for h in range(2):
+                    own_on(w, part, sems, dev, d, h).wait_send()
+                pass_on(w, part, sems, dev, d).wait_send()
 
     on_own(rows_sent)
 
@@ -825,6 +880,16 @@
         put(r.uv_out, r.u4)
 
     u_back.wait_send()
+
+
+def hand_over(*refs):
+    half = len(refs) // 2
+    for src, out in zip(refs[:half], refs[half:], strict=True):
+        if len(src.shape) == 1:
+            for j in range(src.shape[0]):
+                out[j] = src[j]
+        else:
+            out[...] = src[...]
 
 
 def rotary_tables(length):
@@ -857,13 +922,15 @@
     specs = [vm] * len(INPUTS)
     specs[INPUTS.index("pos_in")] = pl.BlockSpec(memory_space=pltpu.SMEM)
     specs[INPUTS.index("hid_in")] = pl.BlockSpec(memory_space=pl.ANY)
-    shapes = ((8, 128), (2, 4096), (2, 4096), (8, 64), (8, 64), (64, 512), (64, 512))
+    shapes = ((2,), (2, 4096), (2, 4096), (8, 64), (8, 64), (64, 512), (64, 512))
     cosine, sine = rotary_tables(256)
-    loss, q_grad, p_grad, down_key, down_value, up_key, up_value = pl.pallas_call(
+    outs = (vm,) * len(shapes)
+    outs = (pl.BlockSpec(memory_space=pltpu.SMEM), *outs[1:])
+    results = pl.pallas_call(
         kernel,
         out_shape=tuple(jax.ShapeDtypeStruct(shape, F32) for shape in shapes),
         in_specs=specs,
-        out_specs=(vm,) * len(shapes),
+        out_specs=outs,
         scratch_shapes=[pltpu.VMEM(shape, dtype) for shape, dtype in BUFFERS.values()]
         + [pltpu.SemaphoreType.DMA(shape) for shape in SEMAPHORES.values()],
         compiler_params=pltpu.CompilerParams(
@@ -878,15 +945,20 @@
         last_query,
         frozen_key_weight,
         frozen_value_weight,
-        key_down,
+        key_down.T,
         key_adapter_up,
-        value_down,
+        value_down.T,
         value_adapter_up,
         out_weight,
         cosine,
         sine,
     )
-    return (loss[0, :2], q_grad, p_grad, down_key, down_value, up_key, up_value)
+    return pl.pallas_call(
+        hand_over,
+        out_shape=tuple(jax.ShapeDtypeStruct(shape, F32) for shape in shapes),
+        in_specs=outs,
+        out_specs=outs,
+    )(*results)
 
 
 def solution(mesh):

time: 139 us -> 119 us (0.86)
  local copies, waits for them, and re-layouts: 13.8 us -> 1.31 us
  Pallas kernels: 124 us -> 117 us
    unnamed x8 -> x0, local copies, waits for them, and re-layouts: 11.3 us -> none
    pallas_call x1, Pallas kernels: 124 us -> 115 us  [shards(): pl.pallas_call(kernel, out_shape=tuple((jax.ShapeDtypeStruct(shape, F32)...]
    pallas_call x0 -> x1, Pallas kernels: none -> 1.77 us  [shards(): pl.pallas_call(hand_over, out_shape=tuple((jax.ShapeDtypeStruct(shape, F3...]
where the time goes in v3:
time: 119 us
  Pallas kernels  117 us (98%)
  local copies, waits for them, and re-layouts  1.31 us (1%)
    pallas_call x1, Pallas kernels, shards(): pl.pallas_call(kernel, out_shape=tuple((jax.ShapeDtypeStruct(shape, F32)...  115 us

profile of v3, /device:TPU:1, one launch (start us, length us, event | category | flops | bytes accessed | tf_op | source)
XLA Modules:
  0.0 118.5 jit_solution(11331381303316090892)
XLA Ops:
  0.6 1.3 %reshape.21.refs_4_ = bf16[1,4096]{1,0:T(2,128)(2,1)} reshape(bf16[4096]{0:T(1024)(128)(2,1)} %param.19) | data formatting | bytes 16384 | tf_op jit(solution)/shard_map/reshape | solution.py:944
  1.9 114.8 %shard_map.198 = (f32[2]{0:T(128)}, f32[2,4096]{1,0:T(2,128)}, f32[2,4096]{1,0:T(2,128)}, f32[8,64]{1,0:T(8,128)}, f32[8,64]{1,0:T(8,128)}, /*index=5*/f32[64,512]{1,0:T(8,128)}, f32[64,512]{1,0:T(8,128)}) custom-call(bf16[2,4096]{1,0:T(2,128)(2,1)} %refs_0_.1, bf16[2,4096]{1,0:T(2,128)(2,1)} %refs_1_.1, s32[2]{0:T(128)} %refs_2_.1, ...), custom_call_target="tpu_custom_call" | custom-call | tf_op jit(solution)/shard_map/pallas_call | solution.py:929
  116.8 1.8 %shard_map.199 = (f32[2]{0:T(128)}, f32[2,4096]{1,0:T(2,128)}, f32[2,4096]{1,0:T(2,128)}, f32[8,64]{1,0:T(8,128)}, f32[8,64]{1,0:T(8,128)}, /*index=5*/f32[64,512]{1,0:T(8,128)}, f32[64,512]{1,0:T(8,128)}) custom-call(f32[2]{0:T(128)} %get-tuple-element.14.refs_0_, f32[2,4096]{1,0:T(2,128)} %get-tuple-element.15.refs_1_, ...), custom_call_target="tpu_custom_call" | custom-call | tf_op jit(solution)/shard_map/pallas_call | solution.py:956

commit v4 on v3

--- a/solution.py
+++ b/solution.py
@@ -67,6 +67,14 @@
 )
 OUTPUTS = ("loss_out", "qg_out", "pg_out", "dk_out", "dv_out", "uk_out", "uv_out")
 BUFFERS = {
+    "q_v": ((2, 4096), BF16),
+    "p_v": ((2, 4096), BF16),
+    "gain_v": ((4096,), BF16),
+    "lq_v": ((2, 2048), BF16),
+    "downs_v": ((2, 64, 128), BF16),
+    "wo_v": ((128, 128), BF16),
+    "cos_v": ((256, 128), F32),
+    "sin_v": ((256, 128), F32),
     "tmp": ((16, 512), F32),
     "lq": ((2, 16, 128), F32),
     "hid": ((512, 4096), BF16),
@@ -113,10 +121,10 @@
     "u5": ((16, 16, 128), F32),
 }
 SEMAPHORES = {
-    "hid_sem": (1,),
+    "loc": (13,),
     "q1": (2, 4), "q2": (2, 4), "qx": (2, 4),
-    "w1": (2, 4), "w2": (2, 4), "wx": (2, 8),
-    "ax": (2, 4), "ay": (2, 6), "bx": (2, 6), "by": (2, 4),
+    "w1": (2, 4), "w2": (2, 4), "wx": (2, 16),
+    "ax": (2, 8), "ay": (2, 12), "bx": (2, 12), "by": (2, 8),
     "p": (2, 16), "o1": (2, 16), "o2": (2, 16), "o3": (2,),
     "qw": (2, 16), "qwx": (2, 16), "sts": (2, 32),
     "pg": (2, 16), "hp": (2, 16), "qg": (2, 16), "qgc": (2,),
@@ -165,8 +173,37 @@
     def arrived(dst, sems, into):
         remote(dst, dst, sems.at[OUT, into], sems.at[IN, into], sib, f).wait_recv()
 
-    hid_copy = pltpu.make_async_copy(r.hid_in, r.hid, r.hid_sem.at[0])
-    hid_copy.start()
+    piece = pl.ds(pl.multiple_of((y * 2 + xlo) * 16, 16), 16)
+    fetch = [
+        pltpu.make_async_copy(src, dst, r.loc.at[n])
+        for n, (src, dst) in enumerate(
+            (
+                (r.fk_in.at[piece, :], r.wk.at[zh, 0, xhi, y, xlo, :, 0:512]),
+                (r.fv_in.at[piece, :], r.wv.at[zh, 0, xhi, y, xlo]),
+                (r.q_in, r.q_v),
+                (r.p_in, r.p_v),
+                (r.kd_in, r.downs_v.at[0]),
+                (r.vd_in, r.downs_v.at[1]),
+                (r.wo_in, r.wo_v),
+                (r.hid_in, r.hid),
+                (r.gain_in, r.gain_v),
+                (r.lq_in, r.lq_v),
+                (r.cos_in, r.cos_v),
+                (r.sin_in, r.sin_v),
+            )
+        )
+    ]
+
+    @pl.when(c == 0)
+    def _():
+        fetch[0].start()
+
+    @pl.when(c == 1)
+    def _():
+        fetch[1].start()
+
+    for copy in fetch[2:]:
+        copy.start()
     barrier = pltpu.get_barrier_semaphore()
 
     def greet(dev):
@@ -188,8 +225,13 @@
                 r.tmp[j * 8 + k : j * 8 + k + 1, :] = rows[j : j + 1, k * 512 : (k + 1) * 512]
         return r.tmp[...].astype(BF16)
 
-    r.qs[c, zh, zl, :, 0:512] = slab(r.q_in)
-    r.ps[pi] = slab(r.p_in)
+    fetch[2].wait()
+    r.qs[c, zh, zl, :, 0:512] = slab(r.q_v)
+    fetch[3].wait()
+    r.ps[pi] = slab(r.p_v)
+    fetch[4].wait()
+    fetch[5].wait()
+    fetch[6].wait()
     row, lane = iota((16, 128), 0), iota((16, 128), 1)
     mark = jnp.zeros((16, 128), F32)
     for j in range(2):
@@ -198,18 +240,16 @@
         mark = jnp.where((row == j * 8) & (lane == 0), high, mark)
         mark = jnp.where((row == j * 8) & (lane == 1), low, mark)
     r.qs[c, zh, zl, :, 512:640] = mark.astype(BF16)
-    piece = pl.ds(pl.multiple_of((y * 2 + xlo) * 16, 16), 16)
-
     @pl.when(c == 0)
     def _():
-        r.wk[zh, zl, xhi, y, xlo, :, 0:512] = r.fk_in[piece, :]
-        downs = jnp.concatenate([r.kd_in[...], r.vd_in[...]], axis=0).astype(F32)
+        fetch[0].wait()
+        downs = r.downs_v[...].reshape(128, 128).astype(F32)
         r.dn[...] = jnp.transpose(downs).astype(BF16)
-        r.wk[zh, zl, xhi, y, xlo, :, 512:640] = r.dn[piece, :]
+        r.wk[zh, 0, xhi, y, xlo, :, 512:640] = r.dn[piece, :]
 
     @pl.when(c == 1)
     def _():
-        r.wv[zh, zl, xhi, y, xlo] = r.fv_in[piece, :]
+        fetch[1].wait()
 
     pl.semaphore_wait(barrier, 46)
 
@@ -235,7 +275,7 @@
 
     def o1(zp):
         return send(
-            r.wo_in.at[pl.ds(zp * 16, 16), :],
+            r.wo_v.at[pl.ds(zp * 16, 16), :],
             r.ws.at[z % 2, z // 2],
             r.o1,
             zp,
@@ -252,7 +292,7 @@
 
         @pl.when(here)
         def _():
-            r.ws[z % 2, z // 2] = r.wo_in[pl.ds(zp * 16, 16), :]
+            r.ws[z % 2, z // 2] = r.wo_v[pl.ds(zp * 16, 16), :]
 
     loop(0, 8, o1_start)
     loop(1, 4, lambda i: q1(i).start())
@@ -270,71 +310,151 @@
         pl.when(c == 1)(lambda: body(r.wk))
 
     def w1(w, i):
-        own = w.at[zh, zl, xhi, y, xlo]
+        own = w.at[zh, 0, xhi, y, xlo]
         return send(own, own, r.w1, i, 4 - i, far(i))
 
     def w1_start(w):
         loop(1, 4, lambda i: w1(w, i).start())
 
     def w2(w, i):
-        part = w.at[:, zl, xhi, y, xlo]
-        return send(part, part, r.w2, i, 4 - i, near(i))
+        part = w.at[:, 0, xhi, y, xlo]
+        return send(part, w.at[:, 4 - i, xhi, y, xlo], r.w2, i, 4 - i, near(i))
 
     lo_z, hi_z = pl.ds(0, 2), pl.ds(2, 2)
 
-    def ax(w, i):
-        part = w.at[lo_z, :, xhi, y, xlo]
-        return send(part, part, r.ax, i, 4 - i, x_dev(i))
-
-    def by(w, i):
-        part = w.at[hi_z, :, xhi, y, xlo]
-        return send(part, part, r.by, i, 4 - i, y_dev(i))
-
-    def a_part(w, i, h):
-        return w.at[h, :, :, (y + i) % 4]
-
-    def b_part(w, i, h):
+    near_z = (pl.ds(0, 1), pl.ds(1, 3))
+
+    def ax(w, g, i):
+        part = w.at[lo_z, near_z[g], xhi, y, xlo]
+        return send(part, part, r.ax, 4 * g + i, 4 * g + 4 - i, x_dev(i))
+
+    def by(w, g, i):
+        part = w.at[hi_z, near_z[g], xhi, y, xlo]
+        return send(part, part, r.by, 4 * g + i, 4 * g + 4 - i, y_dev(i))
+
+    def a_part(w, g, i, h):
+        return w.at[h, near_z[g], :, (y + i) % 4]
+
+    def b_part(w, g, i, h):
         x = x_of(i)
-        return w.at[2 + h, :, x // 2, :, x % 2]
-
-    def own_on(w, part, sems, dev, d, h):
-        own = part(w, 0, h)
-        return send(own, own, sems, d * 2 + h, d * 2 + h, dev(1 + 2 * d))
-
-    def pass_on(w, part, sems, dev, d):
-        got = part(w, 3 - 2 * d, 1 - d)
-        return send(got, got, sems, 4 + d, 4 + d, dev(1 + 2 * d))
+        return w.at[2 + h, near_z[g], x // 2, :, x % 2]
+
+    def own_on(w, g, part, sems, dev, d, h):
+        own = part(w, g, 0, h)
+        n = 6 * g + d * 2 + h
+        return send(own, own, sems, n, n, dev(1 + 2 * d))
+
+    def pass_on(w, g, part, sems, dev, d):
+        got = part(w, g, 3 - 2 * d, 1 - d)
+        n = 6 * g + 4 + d
+        return send(got, got, sems, n, n, dev(1 + 2 * d))
 
     rings = ((a_part, r.ay, y_dev), (b_part, r.bx, x_dev))
 
-    def wx_a(w, i):
-        part = w.at[lo_z, :, :, (y + i) % 4]
-        return send(part, part, r.wx, i, i, (sib, f))
-
-    def wx_b(w, i):
+    def wx_a(w, g, i):
+        part = w.at[lo_z, near_z[g], :, (y + i) % 4]
+        return send(part, part, r.wx, 8 * g + i, 8 * g + i, (sib, f))
+
+    def wx_b(w, g, i):
         x = x_of(i)
-        part = w.at[hi_z, :, x // 2, :, x % 2]
-        return send(part, part, r.wx, 4 + i, 4 + i, (sib, f))
-
-    pl.when(c == 0)(lambda: w1_start(r.wk))
+        part = w.at[hi_z, near_z[g], x // 2, :, x % 2]
+        return send(part, part, r.wx, 8 * g + 4 + i, 8 * g + 4 + i, (sib, f))
+
+    def first_start(w, g):
+        loop(1, 4, lambda i: ax(w, g, i).start())
+        loop(1, 4, lambda i: by(w, g, i).start())
+
+    def first_done(w, g):
+        def a_done(i):
+            x = x_of(i)
+            arrived(w.at[lo_z, near_z[g], x // 2, y, x % 2], r.ax, 4 * g + i)
+
+        def b_done(i):
+            part = w.at[hi_z, near_z[g], xhi, (y + i) % 4, xlo]
+            arrived(part, r.by, 4 * g + i)
+
+        loop(1, 4, a_done)
+        loop(1, 4, b_done)
+
+    def second_start(w, g):
+        for part, sems, dev in rings:
+            own_on(w, g, part, sems, dev, 0, 1).start()
+            own_on(w, g, part, sems, dev, 1, 0).start()
+        for part, sems, dev in rings:
+            own_on(w, g, part, sems, dev, 0, 0).start()
+            own_on(w, g, part, sems, dev, 1, 1).start()
+        wx_a(w, g, 0).start()
+        wx_b(w, g, 0).start()
+
+    def second_pass(w, g):
+        for part, sems, dev in rings:
+            arrived(part(w, g, 3, 1), sems, 6 * g + 1)
+            pass_on(w, g, part, sems, dev, 0).start()
+            arrived(part(w, g, 1, 0), sems, 6 * g + 2)
+            pass_on(w, g, part, sems, dev, 1).start()
+
+    def second_done(w, g):
+        for (part, sems, dev), cross in zip(rings, (wx_a, wx_b)):
+            arrived(part(w, g, 3, 0), sems, 6 * g)
+            cross(w, g, 3).start()
+            arrived(part(w, g, 1, 1), sems, 6 * g + 3)
+            cross(w, g, 1).start()
+        for (part, sems, dev), cross in zip(rings, (wx_a, wx_b)):
+            arrived(part(w, g, 2, 1), sems, 6 * g + 4)
+            arrived(part(w, g, 2, 0), sems, 6 * g + 5)
+            cross(w, g, 2).start()
+
+    def cross_a_done(w):
+        for g in range(2):
+            loop(
+                0,
+                4,
+                lambda i: arrived(
+                    w.at[lo_z, near_z[g], :, (y + i) % 4], r.wx, 8 * g + i
+                ),
+            )
+
+    def cross_b_done(w):
+        for g in range(2):
+
+            def one(i):
+                x = x_of(i)
+                part = w.at[hi_z, near_z[g], x // 2, :, x % 2]
+                arrived(part, r.wx, 8 * g + 4 + i)
+
+            loop(0, 4, one)
+
+    def keys_core(body, g):
+        pl.when(c == 0)(lambda: body(r.wk, g))
+
+    def values_core(body, g):
+        pl.when(c == 1)(lambda: body(r.wv, g))
+
+    def each_core(body, g):
+        keys_core(body, g)
+        values_core(body, g)
+
+    on_own(w1_start)
     loop(1, 16, lambda i: p_move(i).start())
 
     r.ku[0:64, :] = r.ku_in[...]
     r.ku[64:128, :] = jnp.zeros((64, 512), BF16)
     r.vu[0:64, :] = jnp.zeros((64, 512), BF16)
     r.vu[64:128, :] = r.vu_in[...]
-    wide_q = r.lq_in[...].astype(F32)
+    fetch[9].wait()
+    wide_q = r.lq_v[...].astype(F32)
     for j in range(2):
         for h in range(16):
             r.lq[j, h : h + 1, :] = wide_q[j : j + 1, h * 128 : (h + 1) * 128]
 
-    hid_copy.wait()
+    fetch[7].wait()
+    fetch[8].wait()
 
     def norm(i):
         rows = pl.ds(pl.multiple_of(i * 32, 32), 32)
         x = r.hid[rows, :].astype(F32)
         scale = lax.rsqrt(jnp.mean(x * x, axis=1, keepdims=True) + EPSILON)
-        r.hid[rows, :] = (x * scale * r.gain_in[...].astype(F32)).astype(BF16)
+        r.hid[rows, :] = (x * scale * r.gain_v[...].astype(F32).reshape(1, 4096)).astype(BF16)
 
     loop(0, 8, norm)
     loop(1, 4, lambda i: arrived(r.qs.at[c, (zh + i) % 4, zl], r.q1, i))
@@ -360,11 +480,11 @@
         r.wg[:, xhi, :, pl.ds((c * 4 + y) * 16, 16), :] = r.ws[...]
 
     def w1_done(w):
-        loop(1, 4, lambda i: arrived(w.at[(zh + i) % 4, zl, xhi, y, xlo], r.w1, i))
+        loop(1, 4, lambda i: arrived(w.at[(zh + i) % 4, 0, xhi, y, xlo], r.w1, i))
         loop(1, 4, lambda i: w2(w, i).start())
 
-    pl.when(c == 0)(lambda: w1_done(r.wk))
-    pl.when(c == 1)(lambda: w1_start(r.wv))
+    on_own(w1_done)
+    each_core(first_start, 0)
     loop(8, 16, norm)
 
     def q2_done(i):
@@ -374,67 +494,12 @@
     loop(1, 4, q2_done)
 
     def w2_done(w):
-        loop(1, 4, lambda i: arrived(w.at[:, (zl + i) % 4, xhi, y, xlo], r.w2, i))
-
-    def first_start(w):
-        loop(1, 4, lambda i: ax(w, i).start())
-        loop(1, 4, lambda i: by(w, i).start())
-
-    def first_done(w):
-        def a_done(i):
-            x = x_of(i)
-            arrived(w.at[lo_z, :, x // 2, y, x % 2], r.ax, i)
-
-        loop(1, 4, a_done)
-        loop(1, 4, lambda i: arrived(w.at[hi_z, :, xhi, (y + i) % 4, xlo], r.by, i))
-
-    def second_start(w):
-        for part, sems, dev in rings:
-            own_on(w, part, sems, dev, 0, 1).start()
-            own_on(w, part, sems, dev, 1, 0).start()
-        for part, sems, dev in rings:
-            own_on(w, part, sems, dev, 0, 0).start()
-            own_on(w, part, sems, dev, 1, 1).start()
-        wx_a(w, 0).start()
-        wx_b(w, 0).start()
-
-    def second_pass(w):
-        for part, sems, dev in rings:
-            arrived(part(w, 3, 1), sems, 1)
-            pass_on(w, part, sems, dev, 0).start()
-            arrived(part(w, 1, 0), sems, 2)
-            pass_on(w, part, sems, dev, 1).start()
-
-    def second_done(w):
-        for (part, sems, dev), cross in zip(rings, (wx_a, wx_b)):
-            arrived(part(w, 3, 0), sems, 0)
-            cross(w, 3).start()
-            arrived(part(w, 1, 1), sems, 3)
-            cross(w, 1).start()
-        for (part, sems, dev), cross in zip(rings, (wx_a, wx_b)):
-            arrived(part(w, 2, 1), sems, 4)
-            arrived(part(w, 2, 0), sems, 5)
-            cross(w, 2).start()
-
-    def cross_a_done(w):
-        loop(0, 4, lambda i: arrived(w.at[lo_z, :, :, (y + i) % 4], r.wx, i))
-
-    def cross_b_done(w):
-        def one(i):
-            x = x_of(i)
-            arrived(w.at[hi_z, :, x // 2, :, x % 2], r.wx, 4 + i)
-
-        loop(0, 4, one)
-
-    def keys_core(body):
-        pl.when(c == 0)(lambda: body(r.wk))
-
-    def values_core(body):
-        pl.when(c == 1)(lambda: body(r.wv))
-
-    keys_core(w2_done)
-    keys_core(first_start)
-    values_core(w1_done)
+        loop(1, 4, lambda i: arrived(w.at[:, i, xhi, y, xlo], r.w2, i))
+
+    each_core(first_done, 0)
+    each_core(second_start, 0)
+    on_own(w2_done)
+    keys_core(first_start, 1)
 
     def p_done(i):
         t = (pi + i) % 16
@@ -484,10 +549,10 @@
     loop(0, 8, o2_done)
     o3 = remote(half, half, r.o3.at[0], r.o3.at[1], sib, f)
     o3.start()
-    keys_core(first_done)
-    keys_core(second_start)
-    values_core(w2_done)
-    values_core(first_start)
+    each_core(second_pass, 0)
+    keys_core(first_done, 1)
+    keys_core(second_start, 1)
+    values_core(first_start, 1)
     remote(other, other, r.o3.at[0], r.o3.at[1], sib, f).wait_recv()
     q_half = r.qs[c].reshape(256, 640)
     prod = jnp.zeros((256, 1024), F32)
@@ -511,7 +576,8 @@
     loop(1, 16, lambda i: qw_move(i).start())
     qw_cross(z).start()
 
-    keys_core(second_pass)
+    each_core(second_done, 0)
+    keys_core(second_pass, 1)
     def st_done(i):
         s = (line + i) % 32
         arrived(r.st.at[s], r.sts, s)
@@ -550,15 +616,14 @@
 
     loop(1, 16, lambda i: hp_move(i).start())
     r.hpr[pi] = r.hps[pi]
-    values_core(first_done)
-    values_core(second_start)
+    values_core(first_done, 1)
+    values_core(second_start, 1)
     rows8 = (iota((256, 32), 0) // 8 == iota((256, 32), 1)).astype(BF16)
     cols8 = (iota((64, 512), 1) // 8 == iota((64, 512), 0)).astype(BF16)
     spread = dot(dot(rows8, weights).astype(BF16), cols8)
     diag = iota((256, 512), 0) % 8 == iota((256, 512), 1) % 8
     spread = jnp.where(diag, spread, 0.0).astype(BF16)
     r.pgs[...] = (SCALE * dot(spread, q_rows)).astype(BF16).reshape(16, 16, 512)
-    loop(1, 16, lambda i: pg_move(i).start())
     r.pgr[pi] = r.pgs[pi]
 
     r.qgs[...] = (SCALE * dot(spread, p_rows, 0, 0)).astype(BF16).reshape(2, 16, 16, 512)
@@ -574,8 +639,8 @@
         zz = (z + far_first(i)) % 16
         return send(r.qgs.at[c, zz], r.qgr.at[z], r.qg, zz, z, z_dev(zz))
 
-    keys_core(second_done)
-    values_core(second_pass)
+    keys_core(second_done, 1)
+    values_core(second_pass, 1)
     swap.wait_recv()
     r.qgs[c] = (r.qgs[c].astype(F32) + r.qgx[...].astype(F32)).astype(BF16)
     loop(1, 16, lambda i: qg_move(i).start())
@@ -583,8 +648,12 @@
 
     pl.when(c == 1)(lambda: cross_a_done(r.wk))
     pl.when(c == 1)(lambda: cross_b_done(r.wk))
+    def tokens_of(k):
+        cols = [pl.multiple_of((k * 4 + (zl + j) % 4) * 256, 256) for j in range(4)]
+        return jnp.concatenate([r.hid[:, pl.ds(col, 256)] for col in cols], axis=1)
+
     def project(w, raw, k):
-        tokens = r.hid[:, pl.ds(pl.multiple_of(k * 1024, 1024), 1024)]
+        tokens = tokens_of(k)
         part = dot(tokens, w[k].reshape(1024, w.shape[-1]))
 
         @pl.when(k == 0)
@@ -598,6 +667,8 @@
     loop(0, 4, lambda k: project(r.wk, r.raw_k, k))
     r.low[...] = r.raw_k[:, 512:640].astype(BF16)
     adapted = dot(r.low[...], r.ku[...])
+    fetch[10].wait()
+    fetch[11].wait()
     own_group = iota((16, 512), 0) // 4 == iota((16, 512), 1) // 128
 
     def by_group(rows):
@@ -610,12 +681,13 @@
             col = slice(g * 128, (g + 1) * 128)
             key = r.raw_k[tok, col] + 2.0 * adapted[tok, col]
             turned = pltpu.roll(key, 64, axis=1)
-            r.keys[tok, col] = (key * r.cos_in[...] + turned * r.sin_in[...]).astype(BF16)
+            r.keys[tok, col] = (key * r.cos_v[...] + turned * r.sin_v[...]).astype(BF16)
         sim = dot(queries[j], r.keys[tok, :], 1, 1) * ROOT
         sim = jnp.exp(sim - jnp.max(sim, axis=1, keepdims=True))
         r.att[j] = sim / jnp.sum(sim, axis=1, keepdims=True)
 
-    values_core(second_done)
+    values_core(second_done, 1)
+    loop(1, 16, lambda i: pg_move(i).start())
     def hp_done(i):
         t = (pi + i) % 16
         arrived(r.hpr.at[t], r.hp, t)
@@ -644,7 +716,7 @@
     r.raw_v[...] = 2.0 * dot(r.low[...], r.vu[...])
 
     def project_values(k):
-        tokens = r.hid[:, pl.ds(pl.multiple_of(k * 1024, 1024), 1024)]
+        tokens = tokens_of(k)
         r.raw_v[...] += dot(tokens, r.wv[k].reshape(1024, 512))
 
     pl.when(c == 0)(lambda: cross_a_done(r.wv))
@@ -663,7 +735,7 @@
             col = slice(g * 128, (g + 1) * 128)
             part = turned_grad[:, col]
             turned = pltpu.roll(part, 64, axis=1)
-            r.keys[tok, col] = (part * r.cos_in[...] - turned * r.sin_in[...]).astype(BF16)
+            r.keys[tok, col] = (part * r.cos_v[...] - turned * r.sin_v[...]).astype(BF16)
 
     up_k = (2.0 * dot(r.low[...], r.keys[...], 0, 0)).astype(BF16)
     for k in range(4):
@@ -806,20 +878,22 @@
         def one(i):
             w1(w, i).wait_send()
             w2(w, i).wait_send()
-            ax(w, i).wait_send()
-            by(w, i).wait_send()
+            for g in range(2):
+                ax(w, g, i).wait_send()
+                by(w, g, i).wait_send()
 
         def two(i):
-            wx_a(w, i).wait_send()
-            wx_b(w, i).wait_send()
+            for g in range(2):
+                wx_a(w, g, i).wait_send()
+                wx_b(w, g, i).wait_send()
 
         loop(1, 4, one)
         loop(0, 4, two)
         for part, sems, dev in rings:
-            for d in range(2):
+            for g, d in ((0, 0), (0, 1), (1, 0), (1, 1)):
                 for h in range(2):
-                    own_on(w, part, sems, dev, d, h).wait_send()
-                pass_on(w, part, sems, dev, d).wait_send()
+                    own_on(w, g, part, sems, dev, d, h).wait_send()
+                pass_on(w, g, part, sems, dev, d).wait_send()
 
     on_own(rows_sent)
 
@@ -919,9 +993,10 @@
     out_weight,
 ):
     vm = pl.BlockSpec(memory_space=pltpu.VMEM)
-    specs = [vm] * len(INPUTS)
+    specs = [pl.BlockSpec(memory_space=pl.ANY)] * len(INPUTS)
     specs[INPUTS.index("pos_in")] = pl.BlockSpec(memory_space=pltpu.SMEM)
-    specs[INPUTS.index("hid_in")] = pl.BlockSpec(memory_space=pl.ANY)
+    for name in ("ku_in", "vu_in"):
+        specs[INPUTS.index(name)] = vm
     shapes = ((2,), (2, 4096), (2, 4096), (8, 64), (8, 64), (64, 512), (64, 512))
     cosine, sine = rotary_tables(256)
     outs = (vm,) * len(shapes)
@@ -941,7 +1016,7 @@
         passages,
         positives,
         hidden.reshape(512, 4096),
-        norm_gain.reshape(1, 4096),
+        norm_gain,
         last_query,
         frozen_key_weight,
         frozen_value_weight,

time: 119 us -> 112 us (0.941)
  Pallas kernels: 117 us -> 111 us
  local copies, waits for them, and re-layouts: 1.31 us -> 0 us
    pallas_call x1, Pallas kernels: 115 us -> 109 us  [shards(): pl.pallas_call(kernel, out_shape=tuple((jax.ShapeDtypeStruct(shape, F32)...]
    reshape x1 -> x0, local copies, waits for them, and re-layouts: 1.31 us -> none  [shards(): norm_gain.reshape(1, 4096)]
where the time goes in v4:
time: 112 us; the launch traced here: 111 us
  Pallas kernels  111 us (99%)
    pallas_call x1, Pallas kernels, shards(): pl.pallas_call(kernel, out_shape=tuple((jax.ShapeDtypeStruct(shape, F32)...  109 us

profile of v4, /device:TPU:1, one launch (start us, length us, event | category | flops | bytes accessed | tf_op | source)
XLA Modules:
  0.0 111.5 jit_solution(6408225029671589710)
XLA Ops:
  0.6 109.1 %shard_map.198 = (f32[2]{0:T(128)}, f32[2,4096]{1,0:T(2,128)}, f32[2,4096]{1,0:T(2,128)}, f32[8,64]{1,0:T(8,128)}, f32[8,64]{1,0:T(8,128)}, /*index=5*/f32[64,512]{1,0:T(8,128)}, f32[64,512]{1,0:T(8,128)}) custom-call(bf16[2,4096]{1,0:T(2,128)(2,1)} %refs_0_.1, bf16[2,4096]{1,0:T(2,128)(2,1)} %refs_1_.1, s32[2]{0:T(128)} %refs_2_.1, ...), custom_call_target="tpu_custom_call" | custom-call | tf_op jit(solution)/shard_map/pallas_call | solution.py:1004
  109.7 1.8 %shard_map.199 = (f32[2]{0:T(128)}, f32[2,4096]{1,0:T(2,128)}, f32[2,4096]{1,0:T(2,128)}, f32[8,64]{1,0:T(8,128)}, f32[8,64]{1,0:T(8,128)}, /*index=5*/f32[64,512]{1,0:T(8,128)}, f32[64,512]{1,0:T(8,128)}) custom-call(f32[2]{0:T(128)} %get-tuple-element.14.refs_0_, f32[2,4096]{1,0:T(2,128)} %get-tuple-element.15.refs_1_, ...), custom_call_target="tpu_custom_call" | custom-call | tf_op jit(solution)/shard_map/pallas_call | solution.py:1031

commit v5 on v4

--- a/solution.py
+++ b/solution.py
@@ -117,8 +117,7 @@
     "u2": ((16, 16, 128), BF16),
     "v3": ((16, 128), F32),
     "u3": ((16, 16, 128), F32),
-    "u4": ((16, 16, 128), F32),
-    "u5": ((16, 16, 128), F32),
+    "u4": ((32, 16, 128), F32),
 }
 SEMAPHORES = {
     "loc": (13,),
@@ -129,7 +128,7 @@
     "qw": (2, 16), "qwx": (2, 16), "sts": (2, 32),
     "pg": (2, 16), "hp": (2, 16), "qg": (2, 16), "qgc": (2,),
     "one": (2, 3), "sd2": (2, 16), "sd3": (2, 16),
-    "su2": (2, 16), "su3": (2, 16), "su4": (2, 16),
+    "su2": (2, 16), "su3": (2, 16), "su4": (2, 32),
 }
 
 
@@ -215,7 +214,12 @@
         greet(line_dev(16 + zz))
 
     loop(1, 16, greet_line)
-    loop(1, 16, lambda i: greet(plane_dev((pi + i) % 16)))
+    def greet_plane(i):
+        tb, tf = plane_dev((pi + i) % 16)
+        greet((tb, tf))
+        greet((tb + 1 - 2 * c, tf))
+
+    loop(1, 16, greet_plane)
     greet((sib, f))
 
     def slab(ref):
@@ -251,7 +255,7 @@
     def _():
         fetch[1].wait()
 
-    pl.semaphore_wait(barrier, 46)
+    pl.semaphore_wait(barrier, 61)
 
     def far(i):
         return z_dev((z + 4 * i) % 16)
@@ -641,10 +645,6 @@
 
     keys_core(second_done, 1)
     values_core(second_pass, 1)
-    swap.wait_recv()
-    r.qgs[c] = (r.qgs[c].astype(F32) + r.qgx[...].astype(F32)).astype(BF16)
-    loop(1, 16, lambda i: qg_move(i).start())
-    r.qgr[z] = r.qgs[c, z]
 
     pl.when(c == 1)(lambda: cross_a_done(r.wk))
     pl.when(c == 1)(lambda: cross_b_done(r.wk))
@@ -686,6 +686,10 @@
         sim = jnp.exp(sim - jnp.max(sim, axis=1, keepdims=True))
         r.att[j] = sim / jnp.sum(sim, axis=1, keepdims=True)
 
+    swap.wait_recv()
+    r.qgs[c] = (r.qgs[c].astype(F32) + r.qgx[...].astype(F32)).astype(BF16)
+    loop(1, 16, lambda i: qg_move(i).start())
+    r.qgr[z] = r.qgs[c, z]
     values_core(second_done, 1)
     loop(1, 16, lambda i: pg_move(i).start())
     def hp_done(i):
@@ -841,13 +845,15 @@
         arrived(r.u3.at[t], r.su3, t)
 
     loop(1, 16, u3_done)
-    r.u4[pi] = jnp.sum(r.u3[...], axis=0)
+    up_own = c * 16 + pi
+    r.u4[up_own] = jnp.sum(r.u3[...], axis=0)
 
     def u4_move(i):
-        t = (pi + i) % 16
-        return send(r.u4.at[pi], r.u4.at[pi], r.su4, t, pi, plane_dev(t))
-
-    loop(1, 16, lambda i: u4_move(i).start())
+        t = (up_own + i) % 32
+        dev = (((t % 16) // 2) * 2 + t // 16, z * 2 + t % 2)
+        return send(r.u4.at[up_own], r.u4.at[up_own], r.su4, t, up_own, dev)
+
+    loop(1, 32, lambda i: u4_move(i).start())
 
     def d3_done(zz):
         @pl.when(jnp.logical_not(jnp.logical_and(z // 8 == xhi, zz == z)))
@@ -858,14 +864,6 @@
     down_total = jnp.sum(r.d3[...], axis=0)
     r.dk_out[...] = down_total[:, :64]
     r.dv_out[...] = down_total[:, 64:]
-
-    def u4_done(i):
-        t = (pi + i) % 16
-        arrived(r.u4.at[t], r.su4, t)
-
-    loop(1, 16, u4_done)
-    u_back = send(r.u4, r.u5, r.one, 2, 2, (sib, f))
-    u_back.start()
 
     def z_sent(i):
         q1(i).wait_send()
@@ -922,7 +920,6 @@
         u2_move(i).wait_send()
         d2_move(i).wait_send()
         u3_move(i).wait_send()
-        u4_move(i).wait_send()
 
     loop(1, 16, sixteen_sent)
 
@@ -936,24 +933,18 @@
     loop(0, 16, more_sent)
     loop(1, 32, lambda i: st_move((line + i) % 32).wait_send())
 
-    u_back.wait_recv()
-
-    def put(out, src):
-        full = src[...].reshape(256, 128)
-        for k in range(4):
-            out[:, k * 128 : (k + 1) * 128] = full[k * 64 : (k + 1) * 64]
-
-    @pl.when(c == 0)
-    def _():
-        put(r.uk_out, r.u4)
-        put(r.uv_out, r.u5)
-
-    @pl.when(c == 1)
-    def _():
-        put(r.uk_out, r.u5)
-        put(r.uv_out, r.u4)
-
-    u_back.wait_send()
+    loop(1, 32, lambda i: u4_move(i).wait_send())
+
+    def u4_done(i):
+        t = (up_own + i) % 32
+        arrived(r.u4.at[t], r.su4, t)
+
+    loop(1, 32, u4_done)
+    ups = r.u4[...].reshape(512, 128)
+    for k in range(4):
+        col = slice(k * 128, (k + 1) * 128)
+        r.uk_out[:, col] = ups[k * 64 : (k + 1) * 64]
+        r.uv_out[:, col] = ups[256 + k * 64 : 256 + (k + 1) * 64]
 
 
 def hand_over(*refs):

time: 112 us -> 114 us (1.018)
  the two profiles are of different devices: /device:TPU:1 before, /device:TPU:36 now
where the time goes in v5:
time: 114 us
  Pallas kernels  113 us (99%)
    pallas_call x1, Pallas kernels, shards(): pl.pallas_call(kernel, out_shape=tuple((jax.ShapeDtypeStruct(shape, F32)...  111 us

profile of v5, /device:TPU:36, one launch (start us, length us, event | category | flops | bytes accessed | tf_op | source)
XLA Modules:
  0.0 113.8 jit_solution(10798697733250746180)
XLA Ops:
  0.6 111.3 %shard_map.198 = (f32[2]{0:T(128)}, f32[2,4096]{1,0:T(2,128)}, f32[2,4096]{1,0:T(2,128)}, f32[8,64]{1,0:T(8,128)}, f32[8,64]{1,0:T(8,128)}, /*index=5*/f32[64,512]{1,0:T(8,128)}, f32[64,512]{1,0:T(8,128)}) custom-call(bf16[2,4096]{1,0:T(2,128)(2,1)} %refs_0_.1, bf16[2,4096]{1,0:T(2,128)(2,1)} %refs_1_.1, s32[2]{0:T(128)} %refs_2_.1, ...), custom_call_target="tpu_custom_call" | custom-call | tf_op jit(solution)/shard_map/pallas_call | solution.py:995
  112.0 1.8 %shard_map.199 = (f32[2]{0:T(128)}, f32[2,4096]{1,0:T(2,128)}, f32[2,4096]{1,0:T(2,128)}, f32[8,64]{1,0:T(8,128)}, f32[8,64]{1,0:T(8,128)}, /*index=5*/f32[64,512]{1,0:T(8,128)}, f32[64,512]{1,0:T(8,128)}) custom-call(f32[2]{0:T(128)} %get-tuple-element.14.refs_0_, f32[2,4096]{1,0:T(2,128)} %get-tuple-element.15.refs_1_, ...), custom_call_target="tpu_custom_call" | custom-call | tf_op jit(solution)/shard_map/pallas_call | solution.py:1022
